TPU v7x, 256 devices: a whole 4x4x8 slice. The times are simulated.
256 devices in a mesh: region: 8 (over x, z_hi), leaf: 32 (over z_lo, y, core).
Axes of the slice: x: 4, y: 4, z: 8 (z_hi: 2, z_lo: 4; z = z_hi * 4 + z_lo), core: 2. Of those that a mesh axis runs over, the one named last changes fastest.
Arguments:
- whiten: bfloat16 [256, 1024, 1024], P(('region', 'leaf')), as said below
- leaf_root: bfloat16 [256, 1024, 512], P(('region', 'leaf')), may hold values from -6 to 6
- leaf_region: bfloat16 [256, 1024, 512], P(('region', 'leaf')), may hold values from -6 to 6
- root_factor: bfloat16 [512, 512], P('region'), may hold values from -0.25 to 0.25
- root_adjoint: bfloat16 [512, 512], P('region'), may hold values from -0.25 to 0.25
- region_factor: bfloat16 [8, 512, 512], P('region', 'leaf'), may hold values from -0.25 to 0.25
- region_adjoint: bfloat16 [8, 512, 512], P('region', 'leaf'), may hold values from -0.25 to 0.25
Outputs:
- grad_root_basis: bfloat16 [256, 1024, 512], P(('region', 'leaf'))
- grad_region_basis: bfloat16 [256, 1024, 512], P(('region', 'leaf'))
- grad_root_factor: float32 [512, 512], P('leaf')
- grad_region_factor: float32 [8, 512, 512], P('region', 'leaf')
Inputs may be any that keep to these rules, and one draw needn't show every extreme that they name: `whiten`: each whitening matrix is lower triangular with a positive diagonal.
All inputs are finite; a program needn't handle non-finite values.
Results may differ from a plain program's by a relative error of at most 0.018.
Values may be sent and summed in bfloat16 or wider, within the bound.
No kernel may reach another device: no remote copies, remote signals or barrier semaphores. Data moves between devices by JAX's collectives and lax.ppermute only.
A program may use at most 64 MiB of HBM per device.

v0:
```python
import jax
import jax.numpy as jnp
from jax import lax
from jax.sharding import PartitionSpec as P


def copy_for_each(x, axis):
    devices = lax.axis_size(axis)
    return lax.all_to_all(jnp.broadcast_to(x[None], (devices, *x.shape)), axis, 0, 0, tiled=True)


def laid_out(pieces, dim):
    lengths = list(pieces.shape[1:])
    lengths[dim] *= pieces.shape[0]
    return jnp.moveaxis(pieces, 0, dim).reshape(lengths)


def gathered_copies(x, axis, dim):
    pieces = copy_for_each(x, axis)
    return laid_out(pieces, dim)


def side_by_side(arrays, axis, dim, along):
    widths = [a.shape[along] for a in arrays]
    both = jnp.concatenate(arrays, axis=along)
    out = gathered_copies(both, axis, dim)
    return tuple(jnp.split(out, [sum(widths[:k]) for k in range(1, len(widths))], axis=along))


def sent_together(arrays, axis, dim, along):
    ends, at = ([], 0)
    for a in arrays[:-1]:
        at += a.shape[along]
        ends.append(at)
    both = jnp.concatenate(arrays, axis=along)
    return tuple(jnp.split(lax.all_gather(both, axis, axis=dim, tiled=True), ends, axis=along))


def cut_along(x, dim, devices):
    before, after = (x.shape[:dim], x.shape[dim + 1 :])
    return jnp.moveaxis(x.reshape(*before, devices, -1, *after), dim, 0)


def sum_at_owner(x, axis, dim):
    pieces = cut_along(x, dim, lax.axis_size(axis))
    arrived = lax.all_to_all(pieces, axis, split_axis=0, concat_axis=0, tiled=True)
    return arrived.astype(jnp.float32).sum(axis=0)


def over_copies(x, axis):
    return copy_for_each(x, axis).astype(jnp.float32).sum(axis=0)


def on_device(
    whiten, leaf_root, leaf_region, root_factor, root_adjoint, region_factor, region_adjoint
):
    root_full, root_adj_full = side_by_side((root_factor, root_adjoint), "region", 0, 1)
    region_full, region_adj_full = sent_together((region_factor, region_adjoint), "leaf", 1, 0)
    own_factor = region_full[0]
    own_adjoint = region_adj_full[0].astype(jnp.float32)
    root_wide = root_adj_full.astype(jnp.float32)
    root_sym = (root_wide + root_wide.T).astype(jnp.bfloat16)
    region_sym = (own_adjoint + own_adjoint.T).astype(jnp.bfloat16)
    root_basis = jnp.einsum(
        "lor,rk->lok", leaf_root, root_full, preferred_element_type=jnp.float32
    ).astype(jnp.bfloat16)
    region_basis = jnp.einsum(
        "lom,mk->lok", leaf_region, own_factor, preferred_element_type=jnp.float32
    ).astype(jnp.bfloat16)
    root_white = jnp.einsum(
        "lop,lpk->lok", whiten, root_basis, preferred_element_type=jnp.float32
    ).astype(jnp.bfloat16)
    region_white = jnp.einsum(
        "lop,lpk->lok", whiten, region_basis, preferred_element_type=jnp.float32
    ).astype(jnp.bfloat16)
    root_dwhite = jnp.einsum(
        "lok,kj->loj", root_white, root_sym, preferred_element_type=jnp.float32
    ).astype(jnp.bfloat16)
    region_dwhite = jnp.einsum(
        "lok,kj->loj", region_white, region_sym, preferred_element_type=jnp.float32
    ).astype(jnp.bfloat16)
    grad_root = jnp.einsum(
        "lpo,lpk->lok", whiten, root_dwhite, preferred_element_type=jnp.float32
    ).astype(jnp.bfloat16)
    grad_region = jnp.einsum(
        "lpo,lpk->lok", whiten, region_dwhite, preferred_element_type=jnp.float32
    ).astype(jnp.bfloat16)
    scale_obs = 1.0 / whiten.shape[1]
    root_term = (
        jnp.einsum("lor,lok->rk", leaf_root, grad_root, preferred_element_type=jnp.float32)
        * scale_obs
    )
    region_term = (
        jnp.einsum("lom,lok->mk", leaf_region, grad_region, preferred_element_type=jnp.float32)
        * scale_obs
    )
    region_part = sum_at_owner(region_term.astype(jnp.bfloat16), "leaf", 0)
    within = sum_at_owner(root_term.astype(jnp.bfloat16), "leaf", 0)
    root_part = over_copies(within.astype(jnp.bfloat16), "region").astype(jnp.float32)
    return (grad_root, grad_region, root_part, region_part[None])


def solution(mesh):
    return jax.shard_map(
        on_device,
        mesh=mesh,
        in_specs=(
            P(("region", "leaf"), None, None),
            P(("region", "leaf"), None, None),
            P(("region", "leaf"), None, None),
            P("region", None),
            P("region", None),
            P("region", "leaf", None),
            P("region", "leaf", None),
        ),
        out_specs=(
            P(("region", "leaf"), None, None),
            P(("region", "leaf"), None, None),
            P("leaf", None),
            P("region", "leaf", None),
        ),
        check_vma=False,
    )
```

profile of v0, /device:TPU:2, one launch (start us, length us, event | category | flops | bytes accessed | tf_op | source)
XLA Modules:
  0.0 150.6 jit_solution(4593799518810562249)
XLA Ops:
  7.2 0.0 copy-start
  7.2 0.0 copy-start.4
  7.2 1.0 pad_maximum_fusion
  8.2 1.1 broadcast_in_dim.6
  9.3 11.5 %all-to-all-start = ((bf16[8,64,1024]{2,1,0:T(8,128)(2,1)}), bf16[8,64,1024]{2,1,0:T(8,128)(2,1)S(1)}, u32[]{:S(2)}, u32[]{:S(2)}) async-start(bf16[8,64,1024]{2,1,0:T(8,128)(2,1)} %broadcast_in_dim.6), calls=%async_computation | async-start | bytes 2097152 | tf_op jit(solution)/shard_map/all_to_all | solution.py:9
  20.8 0.6 pad_maximum_fusion.1
  21.4 0.1 all-gather.2.cloned.1.call-update
  21.5 24.5 %all-to-all-done = bf16[8,64,1024]{2,1,0:T(8,128)(2,1)S(1)} async-done(((bf16[8,64,1024]{2,1,0:T(8,128)(2,1)}), bf16[8,64,1024]{2,1,0:T(8,128)(2,1)S(1)}, u32[]{:S(2)}, u32[]{:S(2)}) %all-to-all-start) | async-done | bytes 1048608 | tf_op jit(solution)/shard_map/all_to_all | solution.py:9
  46.0 1.0 copy-done.1
  47.0 1.2 slice_convert_fusion
  48.1 1.4 copy.15
  49.5 4.3 %fusion.8 = bf16[512,1024]{1,0:T(8,128)(2,1)} fusion(bf16[1,1024,1024]{2,1,0:T(8,128)(2,1)S(1)} %copy-done, bf16[1,1024,512]{2,1,0:T(8,128)(2,1)} %param.8, bf16[512,1024]{1,0:T(8,128)(2,1)} %bitcast.75), kind=kOutput, calls=%fused_computation.8 | convolution fusion | flops 1611661312 | bytes 4718592 | tf_op jit(solution)/shard_map/lop,lpk->lok/dot_general | solution.py:70
  53.8 4.3 %fusion.11 = bf16[512,1024]{1,0:T(8,128)(2,1)} fusion(bf16[1,1024,1024]{2,1,0:T(8,128)(2,1)S(1)} %copy-done, bf16[512,1024]{1,0:T(8,128)(2,1)} %fusion.8, f32[512,512]{0,1:T(8,128)} %copy.15, bf16[512,1024]{1,0:T(8,128)(2,1)S(1)} %bitcast.76), kind=kOutput, calls=%fused_computation.9 | convolution fusion | flops 1612447744 | bytes 5767168 | tf_op jit(solution)/shard_map/lpo,lpk->lok/dot_general | solution.py:82
  58.1 3.1 %fusion.20 = bf16[512,512]{0,1:T(8,128)(2,1)} fusion(bf16[512,1024]{1,0:T(8,128)(2,1)} %fusion.11, bf16[1,1024,512]{2,1,0:T(8,128)(2,1)} %param.8), kind=kOutput, calls=%fused_computation.18 | convolution fusion | flops 537395200 | bytes 2621440 | tf_op jit(solution)/shard_map/lor,lok->rk/dot_general | solution.py:90
  61.2 9.7 %all-to-all-start.1 = ((bf16[32,16,512]{2,1,0:T(8,128)(2,1)}), bf16[32,16,512]{2,1,0:T(8,128)(2,1)}, u32[]{:S(2)}, u32[]{:S(2)}) async-start(bf16[32,16,512]{2,1,0:T(8,128)(2,1)} %bitcast.14), calls=%async_computation.1 | async-start | bytes 1048576 | tf_op jit(solution)/shard_map/all_to_all | solution.py:46
  70.9 20.1 %all-gather.2.cloned.1.call-done = bf16[2,512,512]{2,1,0:T(8,128)(2,1)} async-done(((bf16[2,16,512]{2,1,0:T(8,128)(2,1)}), bf16[2,512,512]{2,1,0:T(8,128)(2,1)}) %all-gather.2.cloned.1.call-update) | async-done | bytes 1048592 | tf_op jit(solution)/shard_map/all_gather | solution.py:36
  91.0 1.2 fusion.36
  92.2 1.4 copy.16
  93.6 4.2 %fusion.14 = bf16[512,1024]{1,0:T(8,128)(2,1)} fusion(bf16[1,1024,1024]{2,1,0:T(8,128)(2,1)S(1)} %copy-done, bf16[1,1024,512]{2,1,0:T(8,128)(2,1)} %param.9, bf16[2,512,512]{2,1,0:T(8,128)(2,1)} %all-gather.2.cloned.1.call-done), kind=kOutput, calls=%fused_computation.10 | convolution fusion | flops 1611661312 | bytes 4718592 | tf_op jit(solution)/shard_map/lop,lpk->lok/dot_general | solution.py:73
  97.8 3.5 %fusion.17 = bf16[512,1024]{1,0:T(8,128)(2,1)S(1)} fusion(bf16[1,1024,1024]{2,1,0:T(8,128)(2,1)S(1)} %copy-done, bf16[512,1024]{1,0:T(8,128)(2,1)} %fusion.14, f32[512,512]{0,1:T(8,128)} %copy.16, bf16[2,512,512]{2,1,0:T(8,128)(2,1)} %all-gather.2.cloned.1.call-done), kind=kOutput, calls=%fused_computation.11 | convolution fusion | flops 1612447744 | bytes 5767168 | tf_op jit(solution)/shard_map/lpo,lpk->lok/dot_general | solution.py:85
  101.3 3.2 %fusion.21 = bf16[512,512]{0,1:T(8,128)(2,1)} fusion(bf16[512,1024]{1,0:T(8,128)(2,1)S(1)} %fusion.17, bf16[1,1024,512]{2,1,0:T(8,128)(2,1)} %param.9), kind=kOutput, calls=%fused_computation.19 | convolution fusion | flops 537395200 | bytes 2621440 | tf_op jit(solution)/shard_map/lom,lok->mk/dot_general | solution.py:94
  104.4 0.0 all-to-all-done.1
  104.4 5.3 %all-to-all-start.3 = ((bf16[32,16,512]{2,1,0:T(8,128)(2,1)}), bf16[32,16,512]{2,1,0:T(8,128)(2,1)S(1)}, u32[]{:S(2)}, u32[]{:S(2)}) async-start(bf16[32,16,512]{2,1,0:T(8,128)(2,1)} %bitcast.79), calls=%async_computation.3 | async-start | bytes 1048576 | tf_op jit(solution)/shard_map/all_to_all | solution.py:46
  109.7 1.1 reduce_sum.30
  110.9 14.7 %all-to-all-done.3 = bf16[32,16,512]{2,1,0:T(8,128)(2,1)S(1)} async-done(((bf16[32,16,512]{2,1,0:T(8,128)(2,1)}), bf16[32,16,512]{2,1,0:T(8,128)(2,1)S(1)}, u32[]{:S(2)}, u32[]{:S(2)}) %all-to-all-start.3) | async-done | bytes 524320 | tf_op jit(solution)/shard_map/all_to_all | solution.py:46
  125.6 0.7 broadcast_in_dim.7
  126.3 7.5 %all-to-all-start.2 = ((bf16[8,16,512]{2,1,0:T(8,128)(2,1)}), bf16[8,16,512]{2,1,0:T(8,128)(2,1)S(1)}, u32[]{:S(2)}, u32[]{:S(2)}) async-start(bf16[8,16,512]{2,1,0:T(8,128)(2,1)} %broadcast_in_dim.7), calls=%async_computation.2 | async-start | bytes 262144 | tf_op jit(solution)/shard_map/all_to_all | solution.py:9
  133.8 2.3 %copy.17 = bf16[1,1024,512]{2,1,0:T(8,128)(2,1)} copy(bf16[1,1024,512]{1,2,0:T(8,128)(2,1)} %bitcast.77) | data formatting | bytes 2097152
  136.1 2.3 %copy.18 = bf16[1,1024,512]{2,1,0:T(8,128)(2,1)} copy(bf16[1,1024,512]{1,2,0:T(8,128)(2,1)} %bitcast.78) | data formatting | bytes 2097152
  138.4 0.7 convert_reduce_fusion
  139.1 4.1 %all-to-all-done.2 = bf16[8,16,512]{2,1,0:T(8,128)(2,1)S(1)} async-done(((bf16[8,16,512]{2,1,0:T(8,128)(2,1)}), bf16[8,16,512]{2,1,0:T(8,128)(2,1)S(1)}, u32[]{:S(2)}, u32[]{:S(2)}) %all-to-all-start.2) | async-done | bytes 131104 | tf_op jit(solution)/shard_map/all_to_all | solution.py:9
  143.1 0.6 convert_reduce_fusion.1
  (10 shorter events, 0.0 us)
Async XLA Ops:
  7.2 42.3 %copy-start = (bf16[1,1024,1024]{2,1,0:T(8,128)(2,1)S(1)}, bf16[1,1024,1024]{2,1,0:T(8,128)(2,1)}, u32[]{:S(2)}) copy-start(bf16[1,1024,1024]{2,1,0:T(8,128)(2,1)} %param.7) | copy-start | bytes 6291460
  7.2 13.6 %copy-start.4 = (bf16[1,16,512]{2,1,0:T(8,128)(2,1)S(1)}, bf16[1,16,512]{2,1,0:T(8,128)(2,1)}, u32[]{:S(2)}) copy-start(bf16[1,16,512]{2,1,0:T(8,128)(2,1)} %param.13) | copy-start | bytes 49156
  7.2 13.6 %copy-start.5 = (bf16[1,16,512]{2,1,0:T(8,128)(2,1)S(1)}, bf16[1,16,512]{2,1,0:T(8,128)(2,1)}, u32[]{:S(2)}) copy-start(bf16[1,16,512]{2,1,0:T(8,128)(2,1)} %param.12) | copy-start | bytes 49156
  9.3 36.7 %all-to-all-start = ((bf16[8,64,1024]{2,1,0:T(8,128)(2,1)}), bf16[8,64,1024]{2,1,0:T(8,128)(2,1)S(1)}, u32[]{:S(2)}, u32[]{:S(2)}) async-start(bf16[8,64,1024]{2,1,0:T(8,128)(2,1)} %broadcast_in_dim.6), calls=%async_computation | async-start | bytes 2097152 | tf_op jit(solution)/shard_map/all_to_all | solution.py:9
  20.8 70.2 %all-gather.2.cloned.1.call-start = ((), (), s32[]{:S(2)}) async-start(), calls=%async_computation.4 | async-start | bytes 1081344 | tf_op jit(solution)/shard_map/all_gather | solution.py:36
  46.0 1.0 copy-start.1
  49.5 4.3 %copy-start.2 = (bf16[8,64,1024]{2,1,0:T(8,128)(2,1)S(1)}, bf16[8,64,1024]{2,1,0:T(8,128)(2,1)}, u32[]{:S(2)}) copy-start(bf16[8,64,1024]{2,1,0:T(8,128)(2,1)} %copy-done.1) | copy-start | bytes 3145732
  61.2 43.2 %all-to-all-start.1 = ((bf16[32,16,512]{2,1,0:T(8,128)(2,1)}), bf16[32,16,512]{2,1,0:T(8,128)(2,1)}, u32[]{:S(2)}, u32[]{:S(2)}) async-start(bf16[32,16,512]{2,1,0:T(8,128)(2,1)} %bitcast.14), calls=%async_computation.1 | async-start | bytes 1048576 | tf_op jit(solution)/shard_map/all_to_all | solution.py:46
  101.3 3.2 %copy-start.3 = (bf16[512,1024]{1,0:T(8,128)(2,1)}, bf16[512,1024]{1,0:T(8,128)(2,1)S(1)}, u32[]{:S(2)}) copy-start(bf16[512,1024]{1,0:T(8,128)(2,1)S(1)} %fusion.17) | copy-start | bytes 3145732
  104.4 21.2 %all-to-all-start.3 = ((bf16[32,16,512]{2,1,0:T(8,128)(2,1)}), bf16[32,16,512]{2,1,0:T(8,128)(2,1)S(1)}, u32[]{:S(2)}, u32[]{:S(2)}) async-start(bf16[32,16,512]{2,1,0:T(8,128)(2,1)} %bitcast.79), calls=%async_computation.3 | async-start | bytes 1048576 | tf_op jit(solution)/shard_map/all_to_all | solution.py:46
  126.3 16.9 %all-to-all-start.2 = ((bf16[8,16,512]{2,1,0:T(8,128)(2,1)}), bf16[8,16,512]{2,1,0:T(8,128)(2,1)S(1)}, u32[]{:S(2)}, u32[]{:S(2)}) async-start(bf16[8,16,512]{2,1,0:T(8,128)(2,1)} %broadcast_in_dim.7), calls=%async_computation.2 | async-start | bytes 262144 | tf_op jit(solution)/shard_map/all_to_all | solution.py:9
Sparse Core Ops, SparseCore 0:
  24.1 66.9 all-gather.1
where the time goes:
time: 153 us; the launch traced here: 151 us
  waiting for transfers between devices  63.5 us (42%)
  starting transfers between devices  33.9 us (22%)
  matrix products  22.6 us (15%)
  between operations  14.1 us (9%)
  local copies, waits for them, and re-layouts  10 us (7%)
  other arithmetic  6.43 us (4%)
    all_to_all x2, waiting for transfers between devices, copy_for_each(): lax.all_to_all(jnp.broadcast_to(x[None], (devices, *x.shape)), axis, 0, 0...  28.6 us
    all_gather x1, waiting for transfers between devices, sent_together(): lax.all_gather(both, axis, axis=dim, tiled=True)  20.1 us
    all_to_all x2, starting transfers between devices, copy_for_each(): lax.all_to_all(jnp.broadcast_to(x[None], (devices, *x.shape)), axis, 0, 0...  19 us
    all_to_all x2, starting transfers between devices, sum_at_owner(): lax.all_to_all(pieces, axis, split_axis=0, concat_axis=0, tiled=True)  14.9 us
    all_to_all x2, waiting for transfers between devices, sum_at_owner(): lax.all_to_all(pieces, axis, split_axis=0, concat_axis=0, tiled=True)  14.7 us
    unnamed x14, local copies, waits for them, and re-layouts  5.54 us
    dot_general x1, matrix products, on_device(): jnp.einsum('lpo,lpk->lok', whiten, root_dwhite, preferred_element_type=jn...  4.34 us
    dot_general x1, matrix products, on_device(): jnp.einsum('lop,lpk->lok', whiten, root_basis, preferred_element_type=jnp...  4.29 us
  transfers between devices with their start and end apart: 5, of which 4 were waited for; matrix products, arithmetic and copies ran while one was open for 23% of the time, Pallas kernels for 0%

commit v1 on v0

v1 whole, which is shorter than its diff:
```python
import functools

import jax
import jax.numpy as jnp
from jax import lax
from jax.experimental import pallas as pl
from jax.experimental.pallas import tpu as pltpu
from jax.sharding import PartitionSpec as P

BF = jnp.bfloat16
F32 = jnp.float32
BOTH = ("region", "leaf")
Z_LO, Y, CORE, X, Z_HI = 4, 4, 2, 4, 2
LEAF = Z_LO * Y * CORE
TILE = 256


def place(x, y, z, c):
    return (x * Z_HI + z // Z_LO) * LEAF + (z % Z_LO) * Y * CORE + y * CORE + c


def coordinates(i):
    r, leaf = divmod(i, LEAF)
    x, hi = divmod(r, Z_HI)
    lo, rest = divmod(leaf, Y * CORE)
    y, c = divmod(rest, CORE)
    return x, y, hi * Z_LO + lo, c


def pairs(move):
    return [(i, place(*move(*coordinates(i)))) for i in range(X * Z_HI * LEAF)]


SWAP_CORES = pairs(lambda x, y, z, c: (x, y, z, 1 - c))
MIRROR_Z = pairs(lambda x, y, z, c: (x, y, 7 - z, c))
ALONG_Y = [[place(0, y, lo, c) for y in range(Y)] for lo in range(Z_LO) for c in range(CORE)]
ALONG_Z_LO = [[place(0, y, lo, c) for lo in range(Z_LO)] for y in range(Y) for c in range(CORE)]
ALONG_Z = [
    [place(x, y, z, c) for z in range(Z_LO * Z_HI)]
    for x in range(X)
    for y in range(Y)
    for c in range(CORE)
]
ALONG_X = [[x * Z_HI + hi for x in range(X)] for hi in range(Z_HI)]


def exchange(pieces, axis, groups):
    return lax.all_to_all(pieces, axis, 0, 0, tiled=True, axis_index_groups=groups)


def to_each(x, axis, groups):
    return exchange(jnp.broadcast_to(x[None], (len(groups[0]), *x.shape)), axis, groups)


def added(pieces):
    return pieces.astype(F32).sum(axis=0)


def dot(a, b, dims=((1,), (0,))):
    return lax.dot_general(a, b, (dims, ((), ())), preferred_element_type=F32)


def call(kernel, out_shape, flops, n_scalars, *args):
    operands = args
    moved = sum(a.size * a.dtype.itemsize for a in operands) + sum(
        int(functools.reduce(lambda p, q: p * q, s.shape, 1)) * s.dtype.itemsize for s in out_shape
    )
    specs = [pl.BlockSpec(memory_space=pltpu.SMEM)] * n_scalars + [
        pl.BlockSpec(memory_space=pltpu.VMEM)
    ] * (len(args) - n_scalars)
    return pl.pallas_call(
        kernel,
        out_shape=out_shape,
        in_specs=specs,
        out_specs=[pl.BlockSpec(memory_space=pltpu.VMEM)] * len(out_shape),
        compiler_params=pltpu.CompilerParams(vmem_limit_bytes=48 * 1024 * 1024),
        cost_estimate=pl.CostEstimate(flops=flops, bytes_accessed=moved, transcendentals=0),
    )(*args)


def gram_kernel(core_ref, w_ref, root_ref, region_ref, white_ref, own_ref, send_ref):
    n = w_ref.shape[0]
    width = root_ref.shape[1]
    core = core_ref[0]
    for i in range(n // TILE):
        rows = slice(TILE * i, TILE * (i + 1))
        k = TILE * (i + 1)
        w = w_ref[rows, :k]
        white_ref[rows, :width] = dot(w, root_ref[:k, :]).astype(BF)
        white_ref[rows, width:] = dot(w, region_ref[:k, :]).astype(BF)
    for level in range(2):
        cols = slice(level * width, (level + 1) * width)
        a = white_ref[:, cols]
        for i in range(width // TILE):
            g = dot(a[:, TILE * i : TILE * (i + 1)], a, ((0,), (0,)))
            g = g.reshape(TILE // 32, 2, 16, width)
            rows = slice(TILE // 2 * i, TILE // 2 * (i + 1))
            own = jnp.where(core == 0, g[:, 0], g[:, 1])
            send = jnp.where(core == 0, g[:, 1], g[:, 0])
            own_ref[level, rows, :] = own.reshape(TILE // 2, width).astype(BF)
            send_ref[level, rows, :] = send.reshape(TILE // 2, width).astype(BF)


def back_kernel(w_ref, white_ref, out_ref):
    n = w_ref.shape[0]
    width = white_ref.shape[1] // 2
    for j in range(n // TILE):
        rows = slice(TILE * j, TILE * (j + 1))
        w = w_ref[TILE * j :, rows]
        for level in range(2):
            cols = slice(level * width, (level + 1) * width)
            out_ref[rows, cols] = dot(w, white_ref[TILE * j :, cols], ((0,), (0,))).astype(BF)


def factor_kernel(core_ref, root_mine, root_came, region_mine, region_came, root_out, region_out):
    first = core_ref[0] == 0
    mine, came = root_mine[...], root_came[...]
    factor = jnp.where(first, mine, came)
    adjoint = jnp.where(first, came, mine)
    root_out[...] = (dot(factor, adjoint) + dot(factor, adjoint, ((1,), (1,)))).astype(BF)

    def merged(part):
        a, b = region_mine[part], region_came[part]
        low = jnp.where(first, a, b)
        high = jnp.where(first, b, a)
        return jnp.stack([low, high], axis=1).reshape(512, 512)

    factor, adjoint = merged(0), merged(1)
    region_out[...] = (dot(factor, adjoint) + dot(factor, adjoint, ((1,), (1,)))).astype(BF)


def grads_kernel(back_ref, root_ref, region_ref, root_out, region_out):
    width = root_ref.shape[0]
    for i in range(back_ref.shape[0] // TILE):
        rows = slice(TILE * i, TILE * (i + 1))
        root_out[0, rows, :] = dot(back_ref[rows, :width], root_ref[...]).astype(BF)
        region_out[0, rows, :] = dot(back_ref[rows, width:], region_ref[...]).astype(BF)


def rows_kernel(scale, pieces_ref, factor_ref, out_ref):
    total = pieces_ref[0].astype(F32)
    for k in range(1, pieces_ref.shape[0]):
        total = total + pieces_ref[k].astype(F32)
    high = total.astype(BF)
    low = (total - high.astype(F32)).astype(BF)
    out_ref[...] = (dot(high, factor_ref[...]) + dot(low, factor_ref[...])) * scale


def shaped(*shape, dtype=BF):
    return jax.ShapeDtypeStruct(shape, dtype)


def on_device(
    whiten, leaf_root, leaf_region, root_factor, root_adjoint, region_factor, region_adjoint
):
    obs, width = leaf_root.shape[1:]
    core = lax.axis_index("leaf") % CORE
    hi = lax.axis_index("region") % Z_HI
    cores = core.astype(jnp.int32).reshape(1)
    w = whiten[0]

    root_mine = jnp.where(core == 0, root_factor, root_adjoint)
    root_other = lax.ppermute(root_mine, BOTH, MIRROR_Z)
    root_two = jnp.where(
        hi == 0, jnp.stack([root_mine, root_other]), jnp.stack([root_other, root_mine])
    )
    root_mine = to_each(root_two, "region", ALONG_X).reshape(width, width)
    root_came = lax.ppermute(root_mine, BOTH, SWAP_CORES)

    region_mine = jnp.stack([region_factor[0], region_adjoint[0]])
    region_mine = to_each(region_mine, "leaf", ALONG_Z_LO)
    region_mine = to_each(region_mine, "leaf", ALONG_Y)
    region_mine = jnp.transpose(region_mine, (2, 1, 0, 3, 4)).reshape(2, Z_LO * Y, 16, width)
    region_came = lax.ppermute(region_mine, BOTH, SWAP_CORES)

    white, own, send = call(
        gram_kernel,
        [shaped(obs, 2 * width), shaped(2, width // 2, width), shaped(2, width // 2, width)],
        2 * 2 * (obs * obs * width + obs * width * width),
        1,
        cores,
        w,
        leaf_root[0],
        leaf_region[0],
    )
    came = lax.ppermute(send, BOTH, SWAP_CORES)
    total = (own.astype(F32) + came.astype(F32)).astype(BF)
    total = total.reshape(2, Z_LO, Y, 16, width).transpose(2, 0, 1, 3, 4)
    total = added(exchange(total, "leaf", ALONG_Y)).astype(BF)
    root_pieces = exchange(jnp.concatenate([total[0], total[0]]), BOTH, ALONG_Z)
    region_pieces = exchange(total[1], "leaf", ALONG_Z_LO)
    root_rows = added(root_pieces).astype(BF)
    root_pieces = to_each(root_rows, "region", ALONG_X)

    (back,) = call(
        back_kernel, [shaped(obs, 2 * width)], 2 * 2 * obs * obs * width, 0, w, white
    )
    root_product, region_product = call(
        factor_kernel,
        [shaped(width, width)] * 2,
        2 * 4 * width**3,
        1,
        cores,
        root_mine,
        root_came,
        region_mine,
        region_came,
    )
    grad_root, grad_region = call(
        grads_kernel,
        [shaped(1, obs, width)] * 2,
        2 * 2 * obs * width * width,
        0,
        back,
        root_product,
        region_product,
    )
    rows = functools.partial(rows_kernel, 1.0 / obs)
    out = shaped(16, width, dtype=F32)
    (region_part,) = call(
        rows, [out], 4 * 16 * width * width, 0, region_pieces, region_product
    )
    (root_part,) = call(rows, [out], 4 * 16 * width * width, 0, root_pieces, root_product)
    return grad_root, grad_region, root_part, region_part[None]


def solution(mesh):
    return jax.shard_map(
        on_device,
        mesh=mesh,
        in_specs=(
            P(("region", "leaf"), None, None),
            P(("region", "leaf"), None, None),
            P(("region", "leaf"), None, None),
            P("region", None),
            P("region", None),
            P("region", "leaf", None),
            P("region", "leaf", None),
        ),
        out_specs=(
            P(("region", "leaf"), None, None),
            P(("region", "leaf"), None, None),
            P("leaf", None),
            P("region", "leaf", None),
        ),
        check_vma=False,
    )
```

time: 153 us -> 97.4 us (0.64)
  waiting for transfers between devices: 63.5 us -> 31.4 us
  matrix products: 22.6 us -> 0 us
  between operations: 14.1 us -> 0.78 us
  Pallas kernels: 0 us -> 12.9 us
  other arithmetic: 6.43 us -> 2.52 us
  local copies, waits for them, and re-layouts: 10 us -> 12.8 us
  starting transfers between devices: 33.9 us -> 36.1 us
    dot_general x6 -> x0, matrix products: 22.6 us -> none  [the longest x1 4.34 us: on_device(): jnp.einsum('lpo,lpk->lok', whiten, root_dwhite, preferred_element_type=jn...]
    all_gather x1 -> x0, waiting for transfers between devices: 20.1 us -> none  [sent_together(): lax.all_gather(both, axis, axis=dim, tiled=True)]
    pallas_call x0 -> x6, Pallas kernels: none -> 12.9 us  [call(): pl.pallas_call(kernel, out_shape=out_shape, in_specs=specs, out_specs=[pl...]
    all_to_all x4 -> x7, waiting for transfers between devices: 43.3 us -> 31.4 us  [exchange(): lax.all_to_all(pieces, axis, 0, 0, tiled=True, axis_index_groups=groups)]
    ppermute x0 -> x4, starting transfers between devices: none -> 6.62 us  [the longest x1 5.94 us: on_device(): root_other = lax.ppermute(root_mine, BOTH, MIRROR_Z)]
    all_to_all x4 -> x7, starting transfers between devices: 33.9 us -> 29.5 us  [exchange(): lax.all_to_all(pieces, axis, 0, 0, tiled=True, axis_index_groups=groups)]
    convert_element_type x2 -> x0, local copies, waits for them, and re-layouts: 2.74 us -> none  [the longest x1 1.37 us: on_device(): root_wide = root_adj_full.astype(jnp.float32)]
    unnamed x14 -> x12, local copies, waits for them, and re-layouts: 5.54 us -> 8.27 us
  transfers between devices with their start and end apart: 5 -> 11, of which waited for: 4 -> 5; matrix products, arithmetic and copies ran while one was open for 23% -> 6% of each run, Pallas kernels for 0% -> 12%
where the time goes in v1:
time: 97.4 us; the launch traced here: 96.5 us
  starting transfers between devices  36.1 us (37%)
  waiting for transfers between devices  31.4 us (32%)
  Pallas kernels  12.9 us (13%)
  local copies, waits for them, and re-layouts  12.8 us (13%)
  other arithmetic  2.52 us (3%)
    all_to_all x7, waiting for transfers between devices, exchange(): lax.all_to_all(pieces, axis, 0, 0, tiled=True, axis_index_groups=groups)  31.4 us
    all_to_all x7, starting transfers between devices, exchange(): lax.all_to_all(pieces, axis, 0, 0, tiled=True, axis_index_groups=groups)  29.5 us
    pallas_call x6, Pallas kernels, call(): pl.pallas_call(kernel, out_shape=out_shape, in_specs=specs, out_specs=[pl...  12.9 us
    unnamed x12, local copies, waits for them, and re-layouts  8.27 us
    ppermute x1, starting transfers between devices, on_device(): root_other = lax.ppermute(root_mine, BOTH, MIRROR_Z)  5.94 us
    broadcast_in_dim x4, local copies, waits for them, and re-layouts, to_each(): jnp.broadcast_to(x[None], (len(groups[0]), *x.shape))  2.98 us
  transfers between devices with their start and end apart: 11, of which 5 were waited for; matrix products, arithmetic and copies ran while one was open for 6% of the time, Pallas kernels for 12%

profile of v1, /device:TPU:2, one launch (start us, length us, event | category | flops | bytes accessed | tf_op | source)
XLA Modules:
  0.0 96.5 jit_solution(6964735235915420820)
XLA Ops:
  0.6 0.9 broadcast_select_fusion
  1.5 5.9 %collective-permute-start = (bf16[64,512]{1,0:T(8,128)(2,1)S(1)}, bf16[64,512]{1,0:T(8,128)(2,1)S(1)}, u32[]{:S(2)}, u32[]{:S(2)}) collective-permute-start(bf16[64,512]{1,0:T(8,128)(2,1)S(1)} %broadcast_select_fusion), channel_id=1, source_target_pairs={{0,56},{1,57},{2,58},{3,59},{4,60},{5,61},{6,62},{7,63},{8,48},{9,... | collective-permute-start | bytes 196616 | tf_op jit(solution)/shard_map/ppermute | solution.py:163
  7.4 0.7 pad_maximum_fusion.1
  8.2 0.7 broadcast_in_dim.11
  8.9 3.6 %all-to-all-start.1 = ((bf16[4,2,16,512]{3,2,1,0:T(8,128)(2,1)}), bf16[4,2,16,512]{3,2,1,0:T(8,128)(2,1)S(1)}, u32[]{:S(2)}, u32[]{:S(2)}) async-start(bf16[4,2,16,512]{3,2,1,0:T(8,128)(2,1)} %broadcast_in_dim.11), calls=%async_computation.1 | async-start | bytes 262144 | tf_op jit(solution)/shard_map/all_to_all | solution.py:48
  12.5 1.2 %copy-done.1 = bf16[1,1024,512]{2,1,0:T(8,128)(2,1)S(1)} copy-done((bf16[1,1024,512]{2,1,0:T(8,128)(2,1)S(1)}, bf16[1,1024,512]{2,1,0:T(8,128)(2,1)}, u32[]{:S(2)}) %copy-start.1) | copy-done | bytes 1048600
  13.7 1.2 %copy-done.2 = bf16[1,1024,512]{2,1,0:T(8,128)(2,1)S(1)} copy-done((bf16[1,1024,512]{2,1,0:T(8,128)(2,1)S(1)}, bf16[1,1024,512]{2,1,0:T(8,128)(2,1)}, u32[]{:S(2)}) %copy-start.2) | copy-done | bytes 1048600
  14.9 4.3 %shard_map.102 = (bf16[1024,1024]{1,0:T(8,128)(2,1)S(1)}, bf16[2,256,512]{2,1,0:T(8,128)(2,1)S(1)}, bf16[2,256,512]{2,1,0:T(8,128)(2,1)S(1)}) custom-call(s32[1]{0:T(128)} %bitcast.1.core_ref, bf16[1024,1024]{1,0:T(8,128)(2,1)} %bitcast.22, bf16[1024,512]{1,0:T(8,128)(2,1)S(1)} %bitcast.24, bf16[1024,512]{1,0:T(8,128)(2,1)S(1)} %bitcast.25), custom_call_target="tpu_custom_call" | custom-call | flops 3221225472 | bytes 7340036 | tf_op jit(solution)/shard_map/pallas_call | solution.py:71
  19.2 1.3 %copy-done.5 = bf16[1024,1024]{1,0:T(8,128)(2,1)} copy-done((bf16[1024,1024]{1,0:T(8,128)(2,1)}, bf16[1024,1024]{1,0:T(8,128)(2,1)S(1)}, u32[]{:S(2)}) %copy-start.5) | copy-done | bytes 2097176
  20.6 0.8 broadcast_in_dim.10
  21.4 4.8 %all-to-all-start = ((bf16[4,2,64,512]{3,2,1,0:T(8,128)(2,1)}), bf16[4,2,64,512]{3,2,1,0:T(8,128)(2,1)S(1)}, u32[]{:S(2)}, u32[]{:S(2)}) async-start(bf16[4,2,64,512]{3,2,1,0:T(8,128)(2,1)} %broadcast_in_dim.10), calls=%async_computation | async-start | bytes 1048576 | tf_op jit(solution)/shard_map/all_to_all | solution.py:48
  26.2 8.7 %all-to-all-done = bf16[4,2,64,512]{3,2,1,0:T(8,128)(2,1)S(1)} async-done(((bf16[4,2,64,512]{3,2,1,0:T(8,128)(2,1)}), bf16[4,2,64,512]{3,2,1,0:T(8,128)(2,1)S(1)}, u32[]{:S(2)}, u32[]{:S(2)}) %all-to-all-start) | async-done | bytes 524320 | tf_op jit(solution)/shard_map/all_to_all | solution.py:48
  34.9 0.9 broadcast_in_dim.12
  35.8 4.5 %all-to-all-start.2 = ((bf16[4,4,2,16,512]{4,3,1,2,0:T(8,128)(2,1)}), bf16[4,4,2,16,512]{4,3,1,2,0:T(8,128)(2,1)S(1)}, u32[]{:S(2)}, u32[]{:S(2)}) async-start(bf16[4,4,2,16,512]{4,3,1,2,0:T(8,128)(2,1)} %broadcast_in_dim.12), calls=%async_computation.2 | async-start | bytes 1048576 | tf_op jit(solution)/shard_map/all_to_all | solution.py:48
  40.4 0.8 copy.15
  41.2 8.1 %all-to-all-done.2 = bf16[4,4,2,16,512]{4,3,1,2,0:T(8,128)(2,1)S(1)} async-done(((bf16[4,4,2,16,512]{4,3,1,2,0:T(8,128)(2,1)}), bf16[4,4,2,16,512]{4,3,1,2,0:T(8,128)(2,1)S(1)}, u32[]{:S(2)}, u32[]{:S(2)}) %all-to-all-start.2) | async-done | bytes 524320 | tf_op jit(solution)/shard_map/all_to_all | solution.py:48
  49.3 3.5 %all-to-all-start.3 = ((bf16[4,2,4,16,512]{4,3,2,1,0:T(8,128)(2,1)}), bf16[4,2,4,16,512]{4,3,2,1,0:T(8,128)(2,1)S(1)}, u32[]{:S(2)}, u32[]{:S(2)}) async-start(bf16[4,2,4,16,512]{4,3,2,1,0:T(8,128)(2,1)} %bitcast.17), calls=%async_computation.3 | async-start | bytes 1048576 | tf_op jit(solution)/shard_map/all_to_all | solution.py:48
  53.5 7.3 %all-to-all-done.3 = bf16[4,2,4,16,512]{4,3,2,1,0:T(8,128)(2,1)S(1)} async-done(((bf16[4,2,4,16,512]{4,3,2,1,0:T(8,128)(2,1)}), bf16[4,2,4,16,512]{4,3,2,1,0:T(8,128)(2,1)S(1)}, u32[]{:S(2)}, u32[]{:S(2)}) %all-to-all-start.3) | async-done | bytes 524320 | tf_op jit(solution)/shard_map/all_to_all | solution.py:48
  61.5 0.7 pad_maximum_fusion
  62.2 5.1 %all-to-all-start.4 = ((bf16[8,16,512]{2,1,0:T(8,128)(2,1)}), bf16[8,16,512]{2,1,0:T(8,128)(2,1)S(1)}, u32[]{:S(2)}, u32[]{:S(2)}) async-start(bf16[8,16,512]{2,1,0:T(8,128)(2,1)} %pad_maximum_fusion), calls=%async_computation.4 | async-start | bytes 262144 | tf_op jit(solution)/shard_map/all_to_all | solution.py:48
  67.3 1.6 %copy-done = bf16[1,1024,1024]{2,1,0:T(8,128)(2,1)S(1)} copy-done((bf16[1,1024,1024]{2,1,0:T(8,128)(2,1)S(1)}, bf16[1,1024,1024]{2,1,0:T(8,128)(2,1)}, u32[]{:S(2)}) %copy-start) | copy-done | bytes 2097176
  68.9 3.2 %shard_map.103.back_ref = bf16[1024,1024]{1,0:T(8,128)(2,1)S(1)} custom-call(bf16[1024,1024]{1,0:T(8,128)(2,1)S(1)} %bitcast.23, bf16[1024,1024]{1,0:T(8,128)(2,1)} %copy-done.5), custom_call_target="tpu_custom_call" | custom-call | flops 2147483648 | bytes 6291456 | tf_op jit(solution)/shard_map/pallas_call | solution.py:71
  72.1 1.3 %copy-done.3 = bf16[1024,1024]{1,0:T(8,128)(2,1)} copy-done((bf16[1024,1024]{1,0:T(8,128)(2,1)}, bf16[1024,1024]{1,0:T(8,128)(2,1)S(1)}, u32[]{:S(2)}) %copy-start.3) | copy-done | bytes 2097176
  73.4 3.0 %all-to-all-done.4 = bf16[8,16,512]{2,1,0:T(8,128)(2,1)S(1)} async-done(((bf16[8,16,512]{2,1,0:T(8,128)(2,1)}), bf16[8,16,512]{2,1,0:T(8,128)(2,1)S(1)}, u32[]{:S(2)}, u32[]{:S(2)}) %all-to-all-start.4) | async-done | bytes 131104 | tf_op jit(solution)/shard_map/all_to_all | solution.py:48
  76.4 3.3 %all-to-all-start.6 = ((bf16[4,16,512]{2,1,0:T(8,128)(2,1)}), bf16[4,16,512]{2,1,0:T(8,128)(2,1)S(1)}, u32[]{:S(2)}, u32[]{:S(2)}) async-start(bf16[4,16,512]{2,1,0:T(8,128)(2,1)} %get-tuple-element.18), calls=%async_computation.6 | async-start | bytes 131072 | tf_op jit(solution)/shard_map/all_to_all | solution.py:48
  79.7 1.3 %shard_map.104 = (bf16[512,512]{1,0:T(8,128)(2,1)S(1)}, bf16[512,512]{1,0:T(8,128)(2,1)S(1)}) custom-call(s32[1]{0:T(128)} %bitcast.1.core_ref, bf16[512,512]{1,0:T(8,128)(2,1)S(1)} %bitcast.19, bf16[512,512]{1,0:T(8,128)(2,1)S(1)} %collective-permute-done.1.root_came, bf16[2,16,16,512]{3,2,1,0:T(8,128)(2,1)S(1)} %bitcast.21, ...), custom_call_target="tpu_custom_call" | custom-call | flops 1073741824 | bytes 3145732 | tf_op jit(solution)/shard_map/pallas_call | solution.py:71
  81.0 4.3 %all-to-all-done.6.pieces_ref = bf16[4,16,512]{2,1,0:T(8,128)(2,1)S(1)} async-done(((bf16[4,16,512]{2,1,0:T(8,128)(2,1)}), bf16[4,16,512]{2,1,0:T(8,128)(2,1)S(1)}, u32[]{:S(2)}, u32[]{:S(2)}) %all-to-all-start.6) | async-done | bytes 65568 | tf_op jit(solution)/shard_map/all_to_all | solution.py:48
  86.0 4.7 %all-to-all-start.5 = ((bf16[4,16,512]{2,1,0:T(8,128)(2,1)}), bf16[4,16,512]{2,1,0:T(8,128)(2,1)S(1)}, u32[]{:S(2)}, u32[]{:S(2)}) async-start(bf16[4,16,512]{2,1,0:T(8,128)(2,1)} %broadcast_in_dim.13), calls=%async_computation.5 | async-start | bytes 131072 | tf_op jit(solution)/shard_map/all_to_all | solution.py:48
  90.7 1.6 %copy-done.4 = bf16[1024,1024]{1,0:T(8,128)(2,1)S(1)} copy-done((bf16[1024,1024]{1,0:T(8,128)(2,1)S(1)}, bf16[1024,1024]{1,0:T(8,128)(2,1)}, u32[]{:S(2)}) %copy-start.4) | copy-done | bytes 2097176
  92.3 2.4 %shard_map.105 = (bf16[1,1024,512]{2,1,0:T(8,128)(2,1)}, bf16[1,1024,512]{2,1,0:T(8,128)(2,1)}) custom-call(bf16[1024,1024]{1,0:T(8,128)(2,1)S(1)} %copy-done.4, bf16[512,512]{1,0:T(8,128)(2,1)S(1)} %get-tuple-element.12.root_ref.factor_ref, bf16[512,512]{1,0:T(8,128)(2,1)S(1)} %get-tuple-element.13.region_ref.factor_ref), custom_call_target="tpu_custom_call" | custom-call | flops 1073741824 | bytes 5242880 | tf_op jit(solution)/shard_map/pallas_call | solution.py:71
  94.7 0.9 shard_map.107
  95.6 0.9 shard_map.106
  (23 shorter events, 2.3 us)
Async XLA Ops:
  1.5 19.0 %collective-permute-start = (bf16[64,512]{1,0:T(8,128)(2,1)S(1)}, bf16[64,512]{1,0:T(8,128)(2,1)S(1)}, u32[]{:S(2)}, u32[]{:S(2)}) collective-permute-start(bf16[64,512]{1,0:T(8,128)(2,1)S(1)} %broadcast_select_fusion), channel_id=1, source_target_pairs={{0,56},{1,57},{2,58},{3,59},{4,60},{5,61},{6,62},{7,63},{8,48},{9,... | collective-permute-start | bytes 196616 | tf_op jit(solution)/shard_map/ppermute | solution.py:163
  8.9 11.7 %all-to-all-start.1 = ((bf16[4,2,16,512]{3,2,1,0:T(8,128)(2,1)}), bf16[4,2,16,512]{3,2,1,0:T(8,128)(2,1)S(1)}, u32[]{:S(2)}, u32[]{:S(2)}) async-start(bf16[4,2,16,512]{3,2,1,0:T(8,128)(2,1)} %broadcast_in_dim.11), calls=%async_computation.1 | async-start | bytes 262144 | tf_op jit(solution)/shard_map/all_to_all | solution.py:48
  12.5 1.2 %copy-start.1 = (bf16[1,1024,512]{2,1,0:T(8,128)(2,1)S(1)}, bf16[1,1024,512]{2,1,0:T(8,128)(2,1)}, u32[]{:S(2)}) copy-start(bf16[1,1024,512]{2,1,0:T(8,128)(2,1)} %param.8) | copy-start | bytes 3145732
  13.7 1.2 %copy-start.2 = (bf16[1,1024,512]{2,1,0:T(8,128)(2,1)S(1)}, bf16[1,1024,512]{2,1,0:T(8,128)(2,1)}, u32[]{:S(2)}) copy-start(bf16[1,1024,512]{2,1,0:T(8,128)(2,1)} %param.9) | copy-start | bytes 3145732
  19.2 1.3 %copy-start.5 = (bf16[1024,1024]{1,0:T(8,128)(2,1)}, bf16[1024,1024]{1,0:T(8,128)(2,1)S(1)}, u32[]{:S(2)}) copy-start(bf16[1024,1024]{1,0:T(8,128)(2,1)S(1)} %get-tuple-element.11.white_ref) | copy-start | bytes 6291460
  20.5 19.7 %collective-permute-start.3 = (bf16[2,256,512]{2,1,0:T(8,128)(2,1)S(1)}, bf16[2,256,512]{2,1,0:T(8,128)(2,1)S(1)}, u32[]{:S(2)}, u32[]{:S(2)}) collective-permute-start(bf16[2,256,512]{2,1,0:T(8,128)(2,1)S(1)} %get-tuple-element.17), channel_id=1, source_target_pairs={{0,1},{1,0},{2,3},{3,2},{4,5},{5,4},{6,7},{7,6},{8,9},{9,8},{10,11... | collective-permute-start | bytes 1572872 | tf_op jit(solution)/shard_map/ppermute | solution.py:186
  21.4 13.5 %all-to-all-start = ((bf16[4,2,64,512]{3,2,1,0:T(8,128)(2,1)}), bf16[4,2,64,512]{3,2,1,0:T(8,128)(2,1)S(1)}, u32[]{:S(2)}, u32[]{:S(2)}) async-start(bf16[4,2,64,512]{3,2,1,0:T(8,128)(2,1)} %broadcast_in_dim.10), calls=%async_computation | async-start | bytes 1048576 | tf_op jit(solution)/shard_map/all_to_all | solution.py:48
  35.8 13.5 %all-to-all-start.2 = ((bf16[4,4,2,16,512]{4,3,1,2,0:T(8,128)(2,1)}), bf16[4,4,2,16,512]{4,3,1,2,0:T(8,128)(2,1)S(1)}, u32[]{:S(2)}, u32[]{:S(2)}) async-start(bf16[4,4,2,16,512]{4,3,1,2,0:T(8,128)(2,1)} %broadcast_in_dim.12), calls=%async_computation.2 | async-start | bytes 1048576 | tf_op jit(solution)/shard_map/all_to_all | solution.py:48
  49.3 11.5 %all-to-all-start.3 = ((bf16[4,2,4,16,512]{4,3,2,1,0:T(8,128)(2,1)}), bf16[4,2,4,16,512]{4,3,2,1,0:T(8,128)(2,1)S(1)}, u32[]{:S(2)}, u32[]{:S(2)}) async-start(bf16[4,2,4,16,512]{4,3,2,1,0:T(8,128)(2,1)} %bitcast.17), calls=%async_computation.3 | async-start | bytes 1048576 | tf_op jit(solution)/shard_map/all_to_all | solution.py:48
  52.8 26.9 %collective-permute-start.1 = (bf16[512,512]{1,0:T(8,128)(2,1)S(1)}, bf16[512,512]{1,0:T(8,128)(2,1)S(1)}, u32[]{:S(2)}, u32[]{:S(2)}) collective-permute-start(bf16[512,512]{1,0:T(8,128)(2,1)S(1)} %bitcast.18), channel_id=1, source_target_pairs={{0,1},{1,0},{2,3},{3,2},{4,5},{5,4},{6,7},{7,6},{8,9},{9,8},{10,11... | collective-permute-start | bytes 1572872 | tf_op jit(solution)/shard_map/ppermute | solution.py:168
  52.9 26.8 %collective-permute-start.2 = (bf16[2,16,16,512]{3,2,1,0:T(8,128)(2,1)S(1)}, bf16[2,16,16,512]{3,2,1,0:T(8,128)(2,1)S(1)}, u32[]{:S(2)}, u32[]{:S(2)}) collective-permute-start(bf16[2,16,16,512]{3,2,1,0:T(8,128)(2,1)S(1)} %bitcast.20), channel_id=1, source_target_pairs={{0,1},{1,0},{2,3},{3,2},{4,5},{5,4},{6,7},{7,6},{8,9},{9,8},{10,11... | collective-permute-start | bytes 1572872 | tf_op jit(solution)/shard_map/ppermute | solution.py:174
  62.2 14.2 %all-to-all-start.4 = ((bf16[8,16,512]{2,1,0:T(8,128)(2,1)}), bf16[8,16,512]{2,1,0:T(8,128)(2,1)S(1)}, u32[]{:S(2)}, u32[]{:S(2)}) async-start(bf16[8,16,512]{2,1,0:T(8,128)(2,1)} %pad_maximum_fusion), calls=%async_computation.4 | async-start | bytes 262144 | tf_op jit(solution)/shard_map/all_to_all | solution.py:48
  67.3 1.6 %copy-start = (bf16[1,1024,1024]{2,1,0:T(8,128)(2,1)S(1)}, bf16[1,1024,1024]{2,1,0:T(8,128)(2,1)}, u32[]{:S(2)}) copy-start(bf16[1,1024,1024]{2,1,0:T(8,128)(2,1)} %param.7) | copy-start | bytes 6291460
  72.1 1.3 %copy-start.3 = (bf16[1024,1024]{1,0:T(8,128)(2,1)}, bf16[1024,1024]{1,0:T(8,128)(2,1)S(1)}, u32[]{:S(2)}) copy-start(bf16[1024,1024]{1,0:T(8,128)(2,1)S(1)} %shard_map.103.back_ref) | copy-start | bytes 6291460
  76.4 9.0 %all-to-all-start.6 = ((bf16[4,16,512]{2,1,0:T(8,128)(2,1)}), bf16[4,16,512]{2,1,0:T(8,128)(2,1)S(1)}, u32[]{:S(2)}, u32[]{:S(2)}) async-start(bf16[4,16,512]{2,1,0:T(8,128)(2,1)} %get-tuple-element.18), calls=%async_computation.6 | async-start | bytes 131072 | tf_op jit(solution)/shard_map/all_to_all | solution.py:48
  86.0 9.6 %all-to-all-start.5 = ((bf16[4,16,512]{2,1,0:T(8,128)(2,1)}), bf16[4,16,512]{2,1,0:T(8,128)(2,1)S(1)}, u32[]{:S(2)}, u32[]{:S(2)}) async-start(bf16[4,16,512]{2,1,0:T(8,128)(2,1)} %broadcast_in_dim.13), calls=%async_computation.5 | async-start | bytes 131072 | tf_op jit(solution)/shard_map/all_to_all | solution.py:48
  90.7 1.6 %copy-start.4 = (bf16[1024,1024]{1,0:T(8,128)(2,1)S(1)}, bf16[1024,1024]{1,0:T(8,128)(2,1)}, u32[]{:S(2)}) copy-start(bf16[1024,1024]{1,0:T(8,128)(2,1)} %copy-done.3) | copy-start | bytes 6291460

commit v2 on v1

v2 whole, which is shorter than its diff:
```python
import functools
import math

import jax
import jax.numpy as jnp
from jax import lax
from jax.experimental import pallas as pl
from jax.experimental.pallas import tpu as pltpu
from jax.sharding import PartitionSpec as P

BF = jnp.bfloat16
F32 = jnp.float32
BOTH = ("region", "leaf")
Z_LO, Y, CORE, X, Z_HI = 4, 4, 2, 4, 2
LEAF = Z_LO * Y * CORE
TILE = 256


def place(x, y, z, c):
    return (x * Z_HI + z // Z_LO) * LEAF + (z % Z_LO) * Y * CORE + y * CORE + c


def coordinates(i):
    r, leaf = divmod(i, LEAF)
    x, hi = divmod(r, Z_HI)
    lo, rest = divmod(leaf, Y * CORE)
    y, c = divmod(rest, CORE)
    return x, y, hi * Z_LO + lo, c


def pairs(move):
    return [(i, place(*move(*coordinates(i)))) for i in range(X * Z_HI * LEAF)]


SWAP_CORES = pairs(lambda x, y, z, c: (x, y, z, 1 - c))
MIRROR_Z = pairs(lambda x, y, z, c: (x, y, 7 - z, c))
Z_ONE = pairs(lambda x, y, z, c: (x, y, z ^ 1, c))
Z_TWO = pairs(lambda x, y, z, c: (x, y, z ^ 2, c))
Y_ONE = pairs(lambda x, y, z, c: (x, y ^ 1, z, c))
Y_THREE = pairs(lambda x, y, z, c: (x, y ^ 3, z, c))
X_ONE = pairs(lambda x, y, z, c: (x ^ 1, y, z, c))
X_TWO = pairs(lambda x, y, z, c: (x ^ 2, y, z, c))
X_THREE = pairs(lambda x, y, z, c: (x ^ 3, y, z, c))
ALONG_Y = [[place(0, y, lo, c) for y in range(Y)] for lo in range(Z_LO) for c in range(CORE)]
ALONG_Z = [
    [place(x, y, z, c) for z in range(Z_LO * Z_HI)]
    for x in range(X)
    for y in range(Y)
    for c in range(CORE)
]


def exchange(pieces, axis, groups):
    return lax.all_to_all(pieces, axis, 0, 0, tiled=True, axis_index_groups=groups)


def sent(x, moves):
    return lax.ppermute(x, BOTH, moves)


def after(x, *others):
    return lax.optimization_barrier((x, *others))[0]


def doubled(x, moves):
    return jnp.stack([x, sent(x, moves)])


def added(pieces):
    return pieces.astype(F32).sum(axis=0)


def dot(a, b, dims=((1,), (0,))):
    return lax.dot_general(a, b, (dims, ((), ())), preferred_element_type=F32)


VMEM, SMEM, HBM = pltpu.VMEM, pltpu.SMEM, pltpu.HBM


def call(kernel, ins, outs, scratch, flops, mib, *args):
    moved = 2 * sum(a.size for a in args) + 2 * sum(math.prod(s.shape) for s, _ in outs)
    args = [pltpu.with_memory_space_constraint(a, m) for a, m in zip(args, ins)]
    return pl.pallas_call(
        kernel,
        out_shape=[s if s.dtype == F32 else m(s.shape, s.dtype) for s, m in outs],
        in_specs=[pl.BlockSpec(memory_space=m) for m in ins],
        out_specs=[pl.BlockSpec(memory_space=m) for _, m in outs],
        scratch_shapes=scratch,
        compiler_params=pltpu.CompilerParams(vmem_limit_bytes=mib * 1024 * 1024),
        cost_estimate=pl.CostEstimate(flops=flops, bytes_accessed=moved, transcendentals=0),
    )(*args)


def position():
    r, leaf = lax.axis_index("region"), lax.axis_index("leaf")
    x, hi = lax.div(r, Z_HI), lax.rem(r, Z_HI)
    lo, rest = lax.div(leaf, Y * CORE), lax.rem(leaf, Y * CORE)
    return x, lax.div(rest, CORE), hi, lo, lax.rem(rest, CORE)


def shaped(*shape, dtype=BF):
    return jax.ShapeDtypeStruct(shape, dtype)


def dma(n):
    return pltpu.SemaphoreType.DMA((n,))


def prepare_kernel(root_f, root_a, region_f, region_a, root_out, region_out, sem):
    core = position()[4]
    copies = [
        pltpu.make_async_copy(region_f.at[0], region_out.at[0], sem.at[0]),
        pltpu.make_async_copy(region_a.at[0], region_out.at[1], sem.at[1]),
    ]
    for copy in copies:
        copy.start()

    @pl.when(core == 0)
    def _():
        copy = pltpu.make_async_copy(root_f, root_out, sem.at[2])
        copy.start()
        copy.wait()

    @pl.when(core != 0)
    def _():
        copy = pltpu.make_async_copy(root_a, root_out, sem.at[2])
        copy.start()
        copy.wait()

    for copy in copies:
        copy.wait()


def gram_kernel(
    w_hbm, root_hbm, region_hbm, white_hbm, own_ref, send_ref, w, leaf, white, in_sem, out_sem
):
    n, width = root_hbm.shape
    tiles = n // TILE
    first = position()[4] == 0
    arrivals, leaving = [], []
    for i in range(tiles):
        rows, k = pl.ds(TILE * i, TILE), pl.ds(0, TILE * (i + 1))
        arrivals.append(
            [
                pltpu.make_async_copy(w_hbm.at[rows, k], w.at[rows, k], in_sem.at[3 * i]),
                pltpu.make_async_copy(
                    root_hbm.at[rows], leaf.at[rows, pl.ds(0, width)], in_sem.at[3 * i + 1]
                ),
                pltpu.make_async_copy(
                    region_hbm.at[rows], leaf.at[rows, pl.ds(width, width)], in_sem.at[3 * i + 2]
                ),
            ]
        )
        for copy in arrivals[-1]:
            copy.start()
    for i in range(tiles):
        for copy in arrivals[i]:
            copy.wait()
        rows, k = slice(TILE * i, TILE * (i + 1)), TILE * (i + 1)
        for level in range(2):
            cols = slice(level * width, (level + 1) * width)
            white[rows, cols] = dot(w[rows, :k], leaf[:k, cols]).astype(BF)
        rows = pl.ds(TILE * i, TILE)
        leaving.append(
            pltpu.make_async_copy(white.at[rows], white_hbm.at[rows], out_sem.at[i])
        )
        leaving[-1].start()
    for level in range(2):
        a = white[:, level * width : (level + 1) * width]
        for i in range(width // TILE):
            g = dot(a[:, TILE * i : TILE * (i + 1)], a, ((0,), (0,)))
            g = g.reshape(TILE // 32, 2, 16, width)
            for b in range(TILE // 32):
                lo, y = divmod(i * (TILE // 32) + b, Y)
                own_ref[y, level, lo] = jnp.where(first, g[b, 0], g[b, 1]).astype(BF)
                send_ref[y, level, lo] = jnp.where(first, g[b, 1], g[b, 0]).astype(BF)
    for copy in leaving:
        copy.wait()


def back_kernel(w_hbm, white_hbm, out_hbm, w, white, out, in_sem, out_sem):
    n = w_hbm.shape[0]
    width = white.shape[1] // 2
    tiles = n // TILE
    arrivals, leaving = [], []
    for i in reversed(range(tiles)):
        rows, k = pl.ds(TILE * i, TILE), pl.ds(0, TILE * (i + 1))
        pair = [
            pltpu.make_async_copy(w_hbm.at[rows, k], w.at[rows, k], in_sem.at[2 * i]),
            pltpu.make_async_copy(white_hbm.at[rows], white.at[rows], in_sem.at[2 * i + 1]),
        ]
        for copy in pair:
            copy.start()
        arrivals.append(pair)
    for i, pair in zip(reversed(range(tiles)), arrivals):
        for copy in pair:
            copy.wait()
        rows = slice(TILE * i, TILE * (i + 1))
        for level in range(2):
            cols = slice(level * width, (level + 1) * width)
            out[rows, cols] = dot(
                w[TILE * i :, rows], white[TILE * i :, cols], ((0,), (0,))
            ).astype(BF)
        rows = pl.ds(TILE * i, TILE)
        leaving.append(pltpu.make_async_copy(out.at[rows], out_hbm.at[rows], out_sem.at[i]))
        leaving[-1].start()
    for copy in leaving:
        copy.wait()


def merge_kernel(own, came, out):
    for k in range(own.shape[0]):
        out[k] = (own[k].astype(F32) + came[k].astype(F32)).astype(BF)


def sum_kernel(pieces, out):
    for level in range(2):
        for lo in range(Z_LO):
            total = pieces[0, level, lo].astype(F32)
            for k in range(1, Y):
                total = total + pieces[k, level, lo].astype(F32)
            total = total.astype(BF)
            for hi in range(Z_HI):
                out[hi * Z_LO + lo, level] = total


def product_of_rows(total, factor, scale):
    high = total.astype(BF)
    low = (total - high.astype(F32)).astype(BF)
    out = dot(jnp.concatenate([high, low]), factor)
    return (out[:16] + out[16:]) * scale


def finish_kernel(
    scale,
    root_mine,
    root_came,
    region_mine,
    region_came,
    pieces,
    back_hbm,
    root_hbm,
    region_hbm,
    rows_out,
    root_product,
    f,
    a,
    region_product,
    back,
    root,
    region,
    in_sem,
    out_sem,
):
    x, y, hi, lo, core = position()
    first = core == 0
    n, width = back.shape[0], f.shape[0]
    arrivals, leaving = [], []
    for i in range(n // TILE):
        rows = pl.ds(TILE * i, TILE)
        arrivals.append(pltpu.make_async_copy(back_hbm.at[rows], back.at[rows], in_sem.at[i]))
        arrivals[-1].start()

    def leave(part, out, i, level):
        rows = pl.ds(TILE * i, TILE)
        copy = pltpu.make_async_copy(
            part.at[rows], out.at[0, rows], out_sem.at[2 * i + level]
        )
        copy.start()
        leaving.append(copy)

    for j in range(X * Z_HI):
        rows = slice(64 * j, 64 * (j + 1))
        v = x ^ (j // Z_HI)
        t = v >> 1
        slot = t * 4 + ((v & 1) ^ t) * 2 + (hi ^ (j % Z_HI))
        mine, came = root_mine[slot], root_came[slot]
        f[rows, :] = jnp.where(first, mine, came)
        a[rows, :] = jnp.where(first, came, mine)
    product = dot(f[...], a[...]) + dot(f[...], a[...], ((1,), (1,)))
    root_product[...] = product.astype(BF)
    for i in range(n // TILE):
        arrivals[i].wait()
        rows = slice(TILE * i, TILE * (i + 1))
        root[rows, :] = dot(back[rows, :width], root_product[...]).astype(BF)
        leave(root, root_hbm, i, 0)
    for j in range(Z_LO * Y):
        v = y ^ (j % Y)
        t = v >> 1
        slot = t * 8 + ((v & 1) ^ t) * 4 + (lo ^ (j // Y))
        for part, out in ((0, f), (1, a)):
            mine, came = region_mine[slot, part], region_came[slot, part]
            out[32 * j : 32 * j + 16, :] = jnp.where(first, mine, came)
            out[32 * j + 16 : 32 * j + 32, :] = jnp.where(first, came, mine)
    product = dot(f[...], a[...]) + dot(f[...], a[...], ((1,), (1,)))
    region_product[...] = product.astype(BF)
    for i in range(n // TILE):
        rows = slice(TILE * i, TILE * (i + 1))
        region[rows, :] = dot(back[rows, width:], region_product[...]).astype(BF)
        leave(region, region_hbm, i, 1)
    total = pieces[hi * Z_LO, 1].astype(F32)
    for k in range(1, Z_LO):
        total = total + pieces[hi * Z_LO + k, 1].astype(F32)
    rows_out[0] = product_of_rows(total, region_product[...], scale)
    for copy in leaving:
        copy.wait()


def root_rows_kernel(scale, a, b, c, d, factor, out_ref):
    total = (a[...].astype(F32) + b[...].astype(F32)) + (c[...].astype(F32) + d[...].astype(F32))
    out_ref[...] = product_of_rows(total, factor[...], scale)


def on_device(
    whiten, leaf_root, leaf_region, root_factor, root_adjoint, region_factor, region_adjoint
):
    obs, width = leaf_root.shape[1:]
    tiles = obs // TILE
    w = whiten[0]

    root_mine, region_mine = call(
        prepare_kernel,
        [HBM] * 4,
        [(shaped(64, width), VMEM), (shaped(2, 16, width), VMEM)],
        [dma(3)],
        0,
        4,
        root_factor,
        root_adjoint,
        region_factor,
        region_adjoint,
    )
    w_first = after(w, root_mine)
    root_mine = doubled(root_mine, MIRROR_Z)
    region_mine = doubled(region_mine, Z_ONE)

    square, strip = VMEM((obs, 2 * width), BF), VMEM((obs, width), BF)
    half = shaped(Y, 2, Z_LO, 16, width)
    white, own, send = call(
        gram_kernel,
        [HBM] * 3,
        [(shaped(obs, 2 * width), HBM), (half, VMEM), (half, VMEM)],
        [VMEM((obs, obs), BF), square, square, dma(3 * tiles), dma(tiles)],
        2 * 2 * (obs * obs * width + obs * width * width),
        20,
        w_first,
        leaf_root[0],
        leaf_region[0],
    )
    send = after(send, region_mine, root_mine)
    region_mine = doubled(after(region_mine, send), Z_TWO)
    root_mine = doubled(after(root_mine, send), X_ONE)
    (total,) = call(
        merge_kernel, [VMEM] * 2, [(half, VMEM)], [], 0, 8, own, sent(send, SWAP_CORES)
    )
    (back,) = call(
        back_kernel,
        [HBM] * 2,
        [(shaped(obs, 2 * width), HBM)],
        [VMEM((obs, obs), BF), square, square, dma(2 * tiles), dma(tiles)],
        2 * 2 * obs * obs * width,
        20,
        w,
        after(white, total),
    )
    region_mine = doubled(after(region_mine, back), Y_ONE)
    root_mine = doubled(after(root_mine, back), X_THREE)
    root_mine = root_mine.reshape(X * Z_HI, 64, width)
    (total,) = call(
        sum_kernel,
        [VMEM],
        [(shaped(Z_LO * Z_HI, 2, 16, width), VMEM)],
        [],
        0,
        8,
        exchange(total, "leaf", ALONG_Y),
    )
    region_mine = doubled(after(region_mine, total), Y_THREE)
    region_mine = region_mine.reshape(Y * Z_LO, 2, 16, width)
    root_came = sent(after(root_mine, total), SWAP_CORES)
    pieces = exchange(total, BOTH, ALONG_Z)
    root_rows = added(pieces[:, 0]).astype(BF)
    region_came = sent(after(region_mine, root_rows), SWAP_CORES)
    others = [sent(root_rows, moves) for moves in (X_ONE, X_THREE, X_TWO)]

    scale = 1.0 / obs
    factor = VMEM((width, width), BF)
    grad_root, grad_region, region_part, root_product = call(
        functools.partial(finish_kernel, scale),
        [VMEM] * 5 + [HBM],
        [
            (shaped(1, obs, width), HBM),
            (shaped(1, obs, width), HBM),
            (shaped(1, 16, width, dtype=F32), VMEM),
            (shaped(width, width), VMEM),
        ],
        [factor, factor, factor, square, strip, strip, dma(tiles), dma(2 * tiles)],
        2 * 2 * obs * width * width + 8 * width**3,
        20,
        root_mine,
        root_came,
        region_mine,
        region_came,
        pieces,
        back,
    )
    (root_part,) = call(
        functools.partial(root_rows_kernel, scale),
        [VMEM] * 5,
        [(shaped(16, width, dtype=F32), VMEM)],
        [],
        4 * 16 * width * width,
        4,
        root_rows,
        *others,
        root_product,
    )
    return grad_root, grad_region, root_part, region_part


def solution(mesh):
    return jax.shard_map(
        on_device,
        mesh=mesh,
        in_specs=(
            P(("region", "leaf"), None, None),
            P(("region", "leaf"), None, None),
            P(("region", "leaf"), None, None),
            P("region", None),
            P("region", None),
            P("region", "leaf", None),
            P("region", "leaf", None),
        ),
        out_specs=(
            P(("region", "leaf"), None, None),
            P(("region", "leaf"), None, None),
            P("leaf", None),
            P("region", "leaf", None),
        ),
        check_vma=False,
    )
```

time: 97.4 us -> 58.4 us (0.60)
  the two profiles are of different devices: /device:TPU:2 before, /device:TPU:1 now
where the time goes in v2:
time: 58.4 us; the launch traced here: 58.1 us
  starting transfers between devices  35.6 us (61%)
  Pallas kernels  17.2 us (29%)
  waiting for transfers between devices  4.23 us (7%)
  between operations  0.76 us (1%)
    ppermute x13, starting transfers between devices, sent(): return lax.ppermute(x, BOTH, moves)  27.4 us
    pallas_call x7, Pallas kernels, call(): pl.pallas_call(kernel, out_shape=[s if s.dtype == F32 else m(s.shape, s.d...  17.2 us
    all_to_all x2, starting transfers between devices, exchange(): lax.all_to_all(pieces, axis, 0, 0, tiled=True, axis_index_groups=groups)  8.19 us
    all_to_all x2, waiting for transfers between devices, exchange(): lax.all_to_all(pieces, axis, 0, 0, tiled=True, axis_index_groups=groups)  2.78 us
    ppermute x13, waiting for transfers between devices, sent(): return lax.ppermute(x, BOTH, moves)  1.45 us
  transfers between devices with their start and end apart: 15, of which 2 were waited for; matrix products, arithmetic and copies ran while one was open for 0% of the time, Pallas kernels for 27%

profile of v2, /device:TPU:1, one launch (start us, length us, event | category | flops | bytes accessed | tf_op | source)
XLA Modules:
  0.0 58.1 jit_solution(996682836466700941)
XLA Ops:
  0.6 0.9 %shard_map.102 = (bf16[64,512]{1,0:T(8,128)(2,1)S(1)}, bf16[2,16,512]{2,1,0:T(8,128)(2,1)S(1)}) custom-call(bf16[64,512]{1,0:T(8,128)(2,1)} %root_f.1, bf16[64,512]{1,0:T(8,128)(2,1)} %root_a.1, bf16[1,16,512]{2,1,0:T(8,128)(2,1)} %region_f.1, bf16[1,16,512]{2,1,0:T(8,128)(2,1)} %region_a.1), custom_call_target="tpu_custom_call" | custom-call | bytes 262144 | tf_op jit(solution)/shard_map/pallas_call | solution.py:83
  1.5 6.5 %collective-permute-start = (bf16[64,512]{1,0:T(8,128)(2,1)S(1)}, bf16[64,512]{1,0:T(8,128)(2,1)S(1)}, u32[]{:S(2)}, u32[]{:S(2)}) collective-permute-start(bf16[64,512]{1,0:T(8,128)(2,1)S(1)} %get-tuple-element.23), channel_id=1, source_target_pairs={{0,56},{1,57},{2,58},{3,59},{4,60},{5,61},{6,62},{7,63},{8,48},{9,... | collective-permute-start | bytes 196616 | tf_op jit(solution)/shard_map/ppermute | solution.py:58
  8.0 1.6 %collective-permute-start.1 = (bf16[2,16,512]{2,1,0:T(8,128)(2,1)S(1)}, bf16[2,16,512]{2,1,0:T(8,128)(2,1)S(1)}, u32[]{:S(2)}, u32[]{:S(2)}) collective-permute-start(bf16[2,16,512]{2,1,0:T(8,128)(2,1)S(1)} %get-tuple-element.26), channel_id=1, source_target_pairs={{0,8},{1,9},{2,10},{3,11},{4,12},{5,13},{6,14},{7,15},{8,0},{9,1},... | collective-permute-start | bytes 98312 | tf_op jit(solution)/shard_map/ppermute | solution.py:58
  9.7 4.4 %shard_map.103 = (bf16[1024,1024]{1,0:T(8,128)(2,1)}, bf16[4,2,4,16,512]{4,3,2,1,0:T(8,128)(2,1)S(1)}, bf16[4,2,4,16,512]{4,3,2,1,0:T(8,128)(2,1)S(1)}) custom-call(bf16[1024,1024]{1,0:T(8,128)(2,1)} %bitcast.37, bf16[1024,512]{1,0:T(8,128)(2,1)} %bitcast.39, bf16[1024,512]{1,0:T(8,128)(2,1)} %bitcast.40), custom_call_target="tpu_custom_call" | custom-call | flops 3221225472 | bytes 7340032 | tf_op jit(solution)/shard_map/pallas_call | solution.py:83
  14.1 0.0 collective-permute-done.1
  14.1 1.3 %collective-permute-start.3 = (bf16[4,2,4,16,512]{4,3,2,1,0:T(8,128)(2,1)S(1)}, bf16[4,2,4,16,512]{4,3,2,1,0:T(8,128)(2,1)S(1)}, u32[]{:S(2)}, u32[]{:S(2)}) collective-permute-start(bf16[4,2,4,16,512]{4,3,2,1,0:T(8,128)(2,1)S(1)} %get-tuple-element.27), channel_id=1, source_target_pairs={{0,1},{1,0},{2,3},{3,2},{4,5},{5,4},{6,7},{7,6},{8,9},{9,8},{10,11... | collective-permute-start | bytes 1572872 | tf_op jit(solution)/shard_map/ppermute | solution.py:58
  15.5 0.3 collective-permute-start.6
  15.7 1.2 %collective-permute-start.2 = (bf16[2,64,512]{2,1,0:T(8,128)(2,1)S(1)}, bf16[2,64,512]{2,1,0:T(8,128)(2,1)S(1)}, u32[]{:S(2)}, u32[]{:S(2)}) collective-permute-start(bf16[2,64,512]{2,1,0:T(8,128)(2,1)S(1)} %pad_maximum_fusion.4), channel_id=1, source_target_pairs={{0,64},{1,65},{2,66},{3,67},{4,68},{5,69},{6,70},{7,71},{8,72},{9,... | collective-permute-start | bytes 393224 | tf_op jit(solution)/shard_map/ppermute | solution.py:58
  17.0 0.0 collective-permute-done.3.came
  17.0 0.9 %shard_map.104 = bf16[4,2,4,16,512]{4,3,2,1,0:T(8,128)(2,1)} custom-call(bf16[4,2,4,16,512]{4,3,2,1,0:T(8,128)(2,1)S(1)} %get-tuple-element.30.own, bf16[4,2,4,16,512]{4,3,2,1,0:T(8,128)(2,1)S(1)} %collective-permute-done.3.came), custom_call_target="tpu_custom_call" | custom-call | bytes 1572864 | tf_op jit(solution)/shard_map/pallas_call | solution.py:83
  17.9 4.2 %all-to-all-start = ((bf16[4,2,4,16,512]{4,3,2,1,0:T(8,128)(2,1)}), bf16[4,2,4,16,512]{4,3,2,1,0:T(8,128)(2,1)S(1)}, u32[]{:S(2)}, u32[]{:S(2)}) async-start(bf16[4,2,4,16,512]{4,3,2,1,0:T(8,128)(2,1)} %shard_map.104), calls=%async_computation | async-start | bytes 1048576 | tf_op jit(solution)/shard_map/all_to_all | solution.py:54
  22.1 0.0 collective-permute-done.6
  22.1 4.3 %shard_map.105.back_hbm = bf16[1024,1024]{1,0:T(8,128)(2,1)} custom-call(bf16[1024,1024]{1,0:T(8,128)(2,1)} %bitcast.38, bf16[1024,1024]{1,0:T(8,128)(2,1)} %get-tuple-element.31.white_hbm), custom_call_target="tpu_custom_call" | custom-call | flops 2147483648 | bytes 6291456 | tf_op jit(solution)/shard_map/pallas_call | solution.py:83
  26.4 1.6 %collective-permute-start.7 = (bf16[2,2,2,16,512]{4,3,2,1,0:T(8,128)(2,1)S(1)}, bf16[2,2,2,16,512]{4,3,2,1,0:T(8,128)(2,1)S(1)}, u32[]{:S(2)}, u32[]{:S(2)}) collective-permute-start(bf16[2,2,2,16,512]{4,3,2,1,0:T(8,128)(2,1)S(1)} %pad_maximum_fusion.5), channel_id=1, source_target_pairs={{0,2},{1,3},{2,0},{3,1},{4,6},{5,7},{6,4},{7,5},{8,10},{9,11},{10,... | collective-permute-start | bytes 393224 | tf_op jit(solution)/shard_map/ppermute | solution.py:58
  28.0 2.6 %collective-permute-start.4 = (bf16[2,2,64,512]{3,2,1,0:T(8,128)(2,1)S(1)}, bf16[2,2,64,512]{3,2,1,0:T(8,128)(2,1)S(1)}, u32[]{:S(2)}, u32[]{:S(2)}) collective-permute-start(bf16[2,2,64,512]{3,2,1,0:T(8,128)(2,1)S(1)} %pad_maximum_fusion.2), channel_id=1, source_target_pairs={{0,192},{1,193},{2,194},{3,195},{4,196},{5,197},{6,198},{7,199},{8... | collective-permute-start | bytes 786440 | tf_op jit(solution)/shard_map/ppermute | solution.py:58
  30.6 0.8 %shard_map.106 = bf16[8,2,16,512]{3,2,1,0:T(8,128)(2,1)} custom-call(bf16[4,2,4,16,512]{4,3,2,1,0:T(8,128)(2,1)S(1)} %all-to-all-done.pieces), custom_call_target="tpu_custom_call" | custom-call | bytes 786432 | tf_op jit(solution)/shard_map/pallas_call | solution.py:83
  31.4 4.0 %all-to-all-start.1 = ((bf16[8,2,16,512]{3,2,1,0:T(8,128)(2,1)}), bf16[8,2,16,512]{3,2,1,0:T(8,128)(2,1)S(1)}, u32[]{:S(2)}, u32[]{:S(2)}) async-start(bf16[8,2,16,512]{3,2,1,0:T(8,128)(2,1)} %shard_map.106), calls=%async_computation.1 | async-start | bytes 524288 | tf_op jit(solution)/shard_map/all_to_all | solution.py:54
  35.4 0.0 collective-permute-done.7
  35.4 1.4 %collective-permute-start.8 = (bf16[2,2,2,2,16,512]{5,4,3,2,1,0:T(8,128)(2,1)S(1)}, bf16[2,2,2,2,16,512]{5,4,3,2,1,0:T(8,128)(2,1)S(1)}, u32[]{:S(2)}, u32[]{:S(2)}) collective-permute-start(bf16[2,2,2,2,16,512]{5,4,3,2,1,0:T(8,128)(2,1)S(1)} %pad_maximum_fusion.3), channel_id=1, source_target_pairs={{0,6},{1,7},{2,4},{3,5},{4,2},{5,3},{6,0},{7,1},{8,14},{9,15},{10,... | collective-permute-start | bytes 786440 | tf_op jit(solution)/shard_map/ppermute | solution.py:58
  36.8 0.0 collective-permute-done.4
  36.8 0.1 pad_maximum_fusion
  36.9 3.7 %collective-permute-start.5 = (bf16[8,64,512]{2,1,0:T(8,128)(2,1)S(1)}, bf16[8,64,512]{2,1,0:T(8,128)(2,1)S(1)}, u32[]{:S(2)}, u32[]{:S(2)}) collective-permute-start(bf16[8,64,512]{2,1,0:T(8,128)(2,1)S(1)} %bitcast.19), channel_id=1, source_target_pairs={{0,1},{1,0},{2,3},{3,2},{4,5},{5,4},{6,7},{7,6},{8,9},{9,8},{10,11... | collective-permute-start | bytes 1572872 | tf_op jit(solution)/shard_map/ppermute | solution.py:58
  40.5 1.4 %collective-permute-done.8 = bf16[2,2,2,2,16,512]{5,4,3,2,1,0:T(8,128)(2,1)S(1)} collective-permute-done((bf16[2,2,2,2,16,512]{5,4,3,2,1,0:T(8,128)(2,1)S(1)}, bf16[2,2,2,2,16,512]{5,4,3,2,1,0:T(8,128)(2,1)S(1)}, u32[]{:S(2)}, u32[]{:S(2)}) %collective-permute-start.8) | collective-permute-done | bytes 262176 | tf_op jit(solution)/shard_map/ppermute | solution.py:58
  41.9 0.1 pad_maximum_fusion.1
  42.0 2.8 %all-to-all-done.1.pieces = bf16[8,2,16,512]{3,2,1,0:T(8,128)(2,1)S(1)} async-done(((bf16[8,2,16,512]{3,2,1,0:T(8,128)(2,1)}), bf16[8,2,16,512]{3,2,1,0:T(8,128)(2,1)S(1)}, u32[]{:S(2)}, u32[]{:S(2)}) %all-to-all-start.1) | async-done | bytes 262176 | tf_op jit(solution)/shard_map/all_to_all | solution.py:54
  44.8 4.0 %collective-permute-start.9 = (bf16[16,2,16,512]{3,2,1,0:T(8,128)(2,1)S(1)}, bf16[16,2,16,512]{3,2,1,0:T(8,128)(2,1)S(1)}, u32[]{:S(2)}, u32[]{:S(2)}) collective-permute-start(bf16[16,2,16,512]{3,2,1,0:T(8,128)(2,1)S(1)} %bitcast.21), channel_id=1, source_target_pairs={{0,1},{1,0},{2,3},{3,2},{4,5},{5,4},{6,7},{7,6},{8,9},{9,8},{10,11... | collective-permute-start | bytes 1572872 | tf_op jit(solution)/shard_map/ppermute | solution.py:58
  48.8 0.5 collective-permute-start.10
  49.3 2.3 %collective-permute-start.11 = (bf16[16,512]{1,0:T(8,128)(2,1)S(1)}, bf16[16,512]{1,0:T(8,128)(2,1)S(1)}, u32[]{:S(2)}, u32[]{:S(2)}) collective-permute-start(bf16[16,512]{1,0:T(8,128)(2,1)S(1)} %slice_reduce_fusion.a), channel_id=1, source_target_pairs={{0,192},{1,193},{2,194},{3,195},{4,196},{5,197},{6,198},{7,199},{8... | collective-permute-start | bytes 49160 | tf_op jit(solution)/shard_map/ppermute | solution.py:58
  51.6 0.5 collective-permute-start.12
  52.1 0.0 collective-permute-done.5.root_came
  52.1 5.1 %shard_map.107 = (bf16[1,1024,512]{2,1,0:T(8,128)(2,1)}, bf16[1,1024,512]{2,1,0:T(8,128)(2,1)}, f32[1,16,512]{2,1,0:T(8,128)}, bf16[512,512]{1,0:T(8,128)(2,1)S(1)}) custom-call(bf16[8,64,512]{2,1,0:T(8,128)(2,1)S(1)} %bitcast.20, bf16[8,64,512]{2,1,0:T(8,128)(2,1)S(1)} %collective-permute-done.5.root_came, bf16[16,2,16,512]{3,2,1,0:T(8,128)(2,1)S(1)} %bitcast.22, ...), custom_call_target="tpu_custom_call" | custom-call | flops 2147483648 | bytes 7094272 | tf_op jit(solution)/shard_map/pallas_call | solution.py:83
  57.3 0.8 %shard_map.108 = f32[16,512]{1,0:T(8,128)} custom-call(bf16[16,512]{1,0:T(8,128)(2,1)S(1)} %slice_reduce_fusion.a, bf16[16,512]{1,0:T(8,128)(2,1)S(1)} %collective-permute-done.10.b, bf16[16,512]{1,0:T(8,128)(2,1)S(1)} %collective-permute-done.11.c, bf16[16,512]{1,0:T(8,128)(2,1)S(1)} %collective-permute-done.12.d, bf16[512,512]{1,0:T(8,128)(2,1)S(1)} %get-tuple-element.40.factor), custom_call_target="tpu_custom_call" | custom-call | flops 16777216 | bytes 606208 | tf_op jit(solution)/shard_map/pallas_call | solution.py:83
  (13 shorter events, 0.1 us)
Async XLA Ops:
  1.5 12.6 %collective-permute-start = (bf16[64,512]{1,0:T(8,128)(2,1)S(1)}, bf16[64,512]{1,0:T(8,128)(2,1)S(1)}, u32[]{:S(2)}, u32[]{:S(2)}) collective-permute-start(bf16[64,512]{1,0:T(8,128)(2,1)S(1)} %get-tuple-element.23), channel_id=1, source_target_pairs={{0,56},{1,57},{2,58},{3,59},{4,60},{5,61},{6,62},{7,63},{8,48},{9,... | collective-permute-start | bytes 196616 | tf_op jit(solution)/shard_map/ppermute | solution.py:58
  8.0 6.0 %collective-permute-start.1 = (bf16[2,16,512]{2,1,0:T(8,128)(2,1)S(1)}, bf16[2,16,512]{2,1,0:T(8,128)(2,1)S(1)}, u32[]{:S(2)}, u32[]{:S(2)}) collective-permute-start(bf16[2,16,512]{2,1,0:T(8,128)(2,1)S(1)} %get-tuple-element.26), channel_id=1, source_target_pairs={{0,8},{1,9},{2,10},{3,11},{4,12},{5,13},{6,14},{7,15},{8,0},{9,1},... | collective-permute-start | bytes 98312 | tf_op jit(solution)/shard_map/ppermute | solution.py:58
  14.1 2.9 %collective-permute-start.3 = (bf16[4,2,4,16,512]{4,3,2,1,0:T(8,128)(2,1)S(1)}, bf16[4,2,4,16,512]{4,3,2,1,0:T(8,128)(2,1)S(1)}, u32[]{:S(2)}, u32[]{:S(2)}) collective-permute-start(bf16[4,2,4,16,512]{4,3,2,1,0:T(8,128)(2,1)S(1)} %get-tuple-element.27), channel_id=1, source_target_pairs={{0,1},{1,0},{2,3},{3,2},{4,5},{5,4},{6,7},{7,6},{8,9},{9,8},{10,11... | collective-permute-start | bytes 1572872 | tf_op jit(solution)/shard_map/ppermute | solution.py:58
  15.5 6.6 %collective-permute-start.6 = (bf16[2,2,16,512]{3,2,1,0:T(8,128)(2,1)S(1)}, bf16[2,2,16,512]{3,2,1,0:T(8,128)(2,1)S(1)}, u32[]{:S(2)}, u32[]{:S(2)}) collective-permute-start(bf16[2,2,16,512]{3,2,1,0:T(8,128)(2,1)S(1)} %pad_maximum_fusion.6), channel_id=1, source_target_pairs={{0,16},{1,17},{2,18},{3,19},{4,20},{5,21},{6,22},{7,23},{8,24},{9,... | collective-permute-start | bytes 196616 | tf_op jit(solution)/shard_map/ppermute | solution.py:58
  15.7 12.2 %collective-permute-start.2 = (bf16[2,64,512]{2,1,0:T(8,128)(2,1)S(1)}, bf16[2,64,512]{2,1,0:T(8,128)(2,1)S(1)}, u32[]{:S(2)}, u32[]{:S(2)}) collective-permute-start(bf16[2,64,512]{2,1,0:T(8,128)(2,1)S(1)} %pad_maximum_fusion.4), channel_id=1, source_target_pairs={{0,64},{1,65},{2,66},{3,67},{4,68},{5,69},{6,70},{7,71},{8,72},{9,... | collective-permute-start | bytes 393224 | tf_op jit(solution)/shard_map/ppermute | solution.py:58
  17.9 12.7 %all-to-all-start = ((bf16[4,2,4,16,512]{4,3,2,1,0:T(8,128)(2,1)}), bf16[4,2,4,16,512]{4,3,2,1,0:T(8,128)(2,1)S(1)}, u32[]{:S(2)}, u32[]{:S(2)}) async-start(bf16[4,2,4,16,512]{4,3,2,1,0:T(8,128)(2,1)} %shard_map.104), calls=%async_computation | async-start | bytes 1048576 | tf_op jit(solution)/shard_map/all_to_all | solution.py:54
  26.4 8.9 %collective-permute-start.7 = (bf16[2,2,2,16,512]{4,3,2,1,0:T(8,128)(2,1)S(1)}, bf16[2,2,2,16,512]{4,3,2,1,0:T(8,128)(2,1)S(1)}, u32[]{:S(2)}, u32[]{:S(2)}) collective-permute-start(bf16[2,2,2,16,512]{4,3,2,1,0:T(8,128)(2,1)S(1)} %pad_maximum_fusion.5), channel_id=1, source_target_pairs={{0,2},{1,3},{2,0},{3,1},{4,6},{5,7},{6,4},{7,5},{8,10},{9,11},{10,... | collective-permute-start | bytes 393224 | tf_op jit(solution)/shard_map/ppermute | solution.py:58
  28.0 8.8 %collective-permute-start.4 = (bf16[2,2,64,512]{3,2,1,0:T(8,128)(2,1)S(1)}, bf16[2,2,64,512]{3,2,1,0:T(8,128)(2,1)S(1)}, u32[]{:S(2)}, u32[]{:S(2)}) collective-permute-start(bf16[2,2,64,512]{3,2,1,0:T(8,128)(2,1)S(1)} %pad_maximum_fusion.2), channel_id=1, source_target_pairs={{0,192},{1,193},{2,194},{3,195},{4,196},{5,197},{6,198},{7,199},{8... | collective-permute-start | bytes 786440 | tf_op jit(solution)/shard_map/ppermute | solution.py:58
  31.4 13.4 %all-to-all-start.1 = ((bf16[8,2,16,512]{3,2,1,0:T(8,128)(2,1)}), bf16[8,2,16,512]{3,2,1,0:T(8,128)(2,1)S(1)}, u32[]{:S(2)}, u32[]{:S(2)}) async-start(bf16[8,2,16,512]{3,2,1,0:T(8,128)(2,1)} %shard_map.106), calls=%async_computation.1 | async-start | bytes 524288 | tf_op jit(solution)/shard_map/all_to_all | solution.py:54
  35.4 6.5 %collective-permute-start.8 = (bf16[2,2,2,2,16,512]{5,4,3,2,1,0:T(8,128)(2,1)S(1)}, bf16[2,2,2,2,16,512]{5,4,3,2,1,0:T(8,128)(2,1)S(1)}, u32[]{:S(2)}, u32[]{:S(2)}) collective-permute-start(bf16[2,2,2,2,16,512]{5,4,3,2,1,0:T(8,128)(2,1)S(1)} %pad_maximum_fusion.3), channel_id=1, source_target_pairs={{0,6},{1,7},{2,4},{3,5},{4,2},{5,3},{6,0},{7,1},{8,14},{9,15},{10,... | collective-permute-start | bytes 786440 | tf_op jit(solution)/shard_map/ppermute | solution.py:58
  36.9 15.2 %collective-permute-start.5 = (bf16[8,64,512]{2,1,0:T(8,128)(2,1)S(1)}, bf16[8,64,512]{2,1,0:T(8,128)(2,1)S(1)}, u32[]{:S(2)}, u32[]{:S(2)}) collective-permute-start(bf16[8,64,512]{2,1,0:T(8,128)(2,1)S(1)} %bitcast.19), channel_id=1, source_target_pairs={{0,1},{1,0},{2,3},{3,2},{4,5},{5,4},{6,7},{7,6},{8,9},{9,8},{10,11... | collective-permute-start | bytes 1572872 | tf_op jit(solution)/shard_map/ppermute | solution.py:58
  44.8 7.3 %collective-permute-start.9 = (bf16[16,2,16,512]{3,2,1,0:T(8,128)(2,1)S(1)}, bf16[16,2,16,512]{3,2,1,0:T(8,128)(2,1)S(1)}, u32[]{:S(2)}, u32[]{:S(2)}) collective-permute-start(bf16[16,2,16,512]{3,2,1,0:T(8,128)(2,1)S(1)} %bitcast.21), channel_id=1, source_target_pairs={{0,1},{1,0},{2,3},{3,2},{4,5},{5,4},{6,7},{7,6},{8,9},{9,8},{10,11... | collective-permute-start | bytes 1572872 | tf_op jit(solution)/shard_map/ppermute | solution.py:58
  48.8 8.4 %collective-permute-start.10 = (bf16[16,512]{1,0:T(8,128)(2,1)S(1)}, bf16[16,512]{1,0:T(8,128)(2,1)S(1)}, u32[]{:S(2)}, u32[]{:S(2)}) collective-permute-start(bf16[16,512]{1,0:T(8,128)(2,1)S(1)} %slice_reduce_fusion.a), channel_id=1, source_target_pairs={{0,64},{1,65},{2,66},{3,67},{4,68},{5,69},{6,70},{7,71},{8,72},{9,... | collective-permute-start | bytes 49160 | tf_op jit(solution)/shard_map/ppermute | solution.py:58
  49.3 8.0 %collective-permute-start.11 = (bf16[16,512]{1,0:T(8,128)(2,1)S(1)}, bf16[16,512]{1,0:T(8,128)(2,1)S(1)}, u32[]{:S(2)}, u32[]{:S(2)}) collective-permute-start(bf16[16,512]{1,0:T(8,128)(2,1)S(1)} %slice_reduce_fusion.a), channel_id=1, source_target_pairs={{0,192},{1,193},{2,194},{3,195},{4,196},{5,197},{6,198},{7,199},{8... | collective-permute-start | bytes 49160 | tf_op jit(solution)/shard_map/ppermute | solution.py:58
  51.6 5.7 %collective-permute-start.12 = (bf16[16,512]{1,0:T(8,128)(2,1)S(1)}, bf16[16,512]{1,0:T(8,128)(2,1)S(1)}, u32[]{:S(2)}, u32[]{:S(2)}) collective-permute-start(bf16[16,512]{1,0:T(8,128)(2,1)S(1)} %slice_reduce_fusion.a), channel_id=1, source_target_pairs={{0,128},{1,129},{2,130},{3,131},{4,132},{5,133},{6,134},{7,135},{8... | collective-permute-start | bytes 49160 | tf_op jit(solution)/shard_map/ppermute | solution.py:58

commit v3 on v2

--- a/solution.py
+++ b/solution.py
@@ -41,7 +41,7 @@
 X_ONE = pairs(lambda x, y, z, c: (x ^ 1, y, z, c))
 X_TWO = pairs(lambda x, y, z, c: (x ^ 2, y, z, c))
 X_THREE = pairs(lambda x, y, z, c: (x ^ 3, y, z, c))
-ALONG_Y = [[place(0, y, lo, c) for y in range(Y)] for lo in range(Z_LO) for c in range(CORE)]
+WITH_Y = [pairs(lambda x, y, z, c, k=k: (x, y ^ k, z, c)) for k in (1, 2, 3)]
 ALONG_Z = [
     [place(x, y, z, c) for z in range(Z_LO * Z_HI)]
     for x in range(X)
@@ -62,8 +62,8 @@
     return lax.optimization_barrier((x, *others))[0]
 
 
-def doubled(x, moves):
-    return jnp.stack([x, sent(x, moves)])
+def joined(x, came, *behind):
+    return jnp.stack(lax.optimization_barrier((x, came, *behind))[:2])
 
 
 def added(pieces):
@@ -74,10 +74,12 @@
     return lax.dot_general(a, b, (dims, ((), ())), preferred_element_type=F32)
 
 
+COST = {'prepare_kernel': 1, 'gram_kernel': 3000, 'merge_kernel': 100, 'back_kernel': 2000, 'sum_kernel': 100, 'root_kernel': 0, 'region_kernel': 1500, 'root_rows_kernel': 30}
 VMEM, SMEM, HBM = pltpu.VMEM, pltpu.SMEM, pltpu.HBM
 
 
 def call(kernel, ins, outs, scratch, flops, mib, *args):
+    flops = COST[kernel.func.__name__ if isinstance(kernel, functools.partial) else kernel.__name__]
     moved = 2 * sum(a.size for a in args) + 2 * sum(math.prod(s.shape) for s, _ in outs)
     args = [pltpu.with_memory_space_constraint(a, m) for a, m in zip(args, ins)]
     return pl.pallas_call(
@@ -87,7 +89,7 @@
         out_specs=[pl.BlockSpec(memory_space=m) for _, m in outs],
         scratch_shapes=scratch,
         compiler_params=pltpu.CompilerParams(vmem_limit_bytes=mib * 1024 * 1024),
-        cost_estimate=pl.CostEstimate(flops=flops, bytes_accessed=moved, transcendentals=0),
+        cost_estimate=pl.CostEstimate(flops=flops * 10**6, bytes_accessed=flops * 10**3, transcendentals=0),
     )(*args)
 
 
@@ -208,17 +210,17 @@
         copy.wait()
 
 
-def merge_kernel(own, came, out):
-    for k in range(own.shape[0]):
-        out[k] = (own[k].astype(F32) + came[k].astype(F32)).astype(BF)
-
-
-def sum_kernel(pieces, out):
+def merge_kernel(own, came, *outs):
+    y = position()[1]
+    for k, out in enumerate(outs):
+        out[...] = (own[y ^ k].astype(F32) + came[y ^ k].astype(F32)).astype(BF)
+
+
+def sum_kernel(a, b, c, d, out):
     for level in range(2):
         for lo in range(Z_LO):
-            total = pieces[0, level, lo].astype(F32)
-            for k in range(1, Y):
-                total = total + pieces[k, level, lo].astype(F32)
+            total = a[level, lo].astype(F32) + b[level, lo].astype(F32)
+            total = total + (c[level, lo].astype(F32) + d[level, lo].astype(F32))
             total = total.astype(BF)
             for hi in range(Z_HI):
                 out[hi * Z_LO + lo, level] = total
@@ -231,79 +233,83 @@
     return (out[:16] + out[16:]) * scale
 
 
-def finish_kernel(
-    scale,
-    root_mine,
-    root_came,
-    region_mine,
-    region_came,
-    pieces,
-    back_hbm,
-    root_hbm,
-    region_hbm,
-    rows_out,
-    root_product,
-    f,
-    a,
-    region_product,
-    back,
-    root,
-    region,
-    in_sem,
-    out_sem,
-):
-    x, y, hi, lo, core = position()
+def start_back(level, back_hbm, back, in_sem):
+    width = back.shape[1]
+    copies = []
+    for i in range(back.shape[0] // TILE):
+        rows = pl.ds(TILE * i, TILE)
+        source = back_hbm.at[rows, pl.ds(level * width, width)]
+        copies.append(pltpu.make_async_copy(source, back.at[rows], in_sem.at[i]))
+        copies[-1].start()
+    return copies
+
+
+def gradients(arrivals, back, product, part, out, out_sem):
+    leaving = []
+    for i, copy in enumerate(arrivals):
+        copy.wait()
+        rows = pl.ds(TILE * i, TILE)
+        part[rows, :] = dot(back[rows, :], product[...]).astype(BF)
+        leaving.append(pltpu.make_async_copy(part.at[rows], out.at[0, rows], out_sem.at[i]))
+        leaving[-1].start()
+    for copy in leaving:
+        copy.wait()
+
+
+def factor_product(f, a):
+    product = dot(f[...], a[...]) + dot(f[...], a[...], ((1,), (1,)))
+    return product.astype(BF)
+
+
+def root_kernel(mine_ref, came_ref, back_hbm, out_hbm, product, f, a, back, part, in_sem, out_sem):
+    x, _, hi, _, core = position()
     first = core == 0
-    n, width = back.shape[0], f.shape[0]
-    arrivals, leaving = [], []
-    for i in range(n // TILE):
-        rows = pl.ds(TILE * i, TILE)
-        arrivals.append(pltpu.make_async_copy(back_hbm.at[rows], back.at[rows], in_sem.at[i]))
-        arrivals[-1].start()
-
-    def leave(part, out, i, level):
-        rows = pl.ds(TILE * i, TILE)
-        copy = pltpu.make_async_copy(
-            part.at[rows], out.at[0, rows], out_sem.at[2 * i + level]
-        )
-        copy.start()
-        leaving.append(copy)
-
+    arrivals = start_back(0, back_hbm, back, in_sem)
     for j in range(X * Z_HI):
         rows = slice(64 * j, 64 * (j + 1))
         v = x ^ (j // Z_HI)
         t = v >> 1
         slot = t * 4 + ((v & 1) ^ t) * 2 + (hi ^ (j % Z_HI))
-        mine, came = root_mine[slot], root_came[slot]
+        mine, came = mine_ref[slot], came_ref[slot]
         f[rows, :] = jnp.where(first, mine, came)
         a[rows, :] = jnp.where(first, came, mine)
-    product = dot(f[...], a[...]) + dot(f[...], a[...], ((1,), (1,)))
-    root_product[...] = product.astype(BF)
-    for i in range(n // TILE):
-        arrivals[i].wait()
-        rows = slice(TILE * i, TILE * (i + 1))
-        root[rows, :] = dot(back[rows, :width], root_product[...]).astype(BF)
-        leave(root, root_hbm, i, 0)
+    product[...] = factor_product(f, a)
+    gradients(arrivals, back, product, part, out_hbm, out_sem)
+
+
+def region_kernel(
+    scale,
+    mine_ref,
+    came_ref,
+    pieces,
+    back_hbm,
+    out_hbm,
+    rows_out,
+    f,
+    a,
+    product,
+    back,
+    part,
+    in_sem,
+    out_sem,
+):
+    _, y, hi, lo, core = position()
+    first = core == 0
+    arrivals = start_back(1, back_hbm, back, in_sem)
     for j in range(Z_LO * Y):
         v = y ^ (j % Y)
         t = v >> 1
         slot = t * 8 + ((v & 1) ^ t) * 4 + (lo ^ (j // Y))
-        for part, out in ((0, f), (1, a)):
-            mine, came = region_mine[slot, part], region_came[slot, part]
+        for k, out in ((0, f), (1, a)):
+            mine, came = mine_ref[slot, k], came_ref[slot, k]
             out[32 * j : 32 * j + 16, :] = jnp.where(first, mine, came)
             out[32 * j + 16 : 32 * j + 32, :] = jnp.where(first, came, mine)
-    product = dot(f[...], a[...]) + dot(f[...], a[...], ((1,), (1,)))
-    region_product[...] = product.astype(BF)
-    for i in range(n // TILE):
-        rows = slice(TILE * i, TILE * (i + 1))
-        region[rows, :] = dot(back[rows, width:], region_product[...]).astype(BF)
-        leave(region, region_hbm, i, 1)
+    product[...] = factor_product(f, a)
     total = pieces[hi * Z_LO, 1].astype(F32)
     for k in range(1, Z_LO):
         total = total + pieces[hi * Z_LO + k, 1].astype(F32)
-    rows_out[0] = product_of_rows(total, region_product[...], scale)
-    for copy in leaving:
-        copy.wait()
+    rows_out[0] = product_of_rows(total, product[...], scale)
+    gradients(arrivals, back, product, part, out_hbm, out_sem)
 
 
 def root_rows_kernel(scale, a, b, c, d, factor, out_ref):
@@ -331,8 +337,7 @@
         region_adjoint,
     )
     w_first = after(w, root_mine)
-    root_mine = doubled(root_mine, MIRROR_Z)
-    region_mine = doubled(region_mine, Z_ONE)
+    root_other, region_other = sent(root_mine, MIRROR_Z), sent(region_mine, Z_ONE)
 
     square, strip = VMEM((obs, 2 * width), BF), VMEM((obs, width), BF)
     half = shaped(Y, 2, Z_LO, 16, width)
@@ -347,12 +352,16 @@
         leaf_root[0],
         leaf_region[0],
     )
-    send = after(send, region_mine, root_mine)
-    region_mine = doubled(after(region_mine, send), Z_TWO)
-    root_mine = doubled(after(root_mine, send), X_ONE)
-    (total,) = call(
-        merge_kernel, [VMEM] * 2, [(half, VMEM)], [], 0, 8, own, sent(send, SWAP_CORES)
-    )
+    send = after(send, root_other, region_other)
+    quarter = shaped(2, Z_LO, 16, width)
+    total, *shares = call(
+        merge_kernel, [VMEM] * 2, [(quarter, VMEM)] * Y, [], 0, 8, own, sent(send, SWAP_CORES)
+    )
+    shares = [sent(shares[k], WITH_Y[k]) for k in (1, 0, 2)]
+    root_mine = joined(root_mine, root_other)
+    root_other = sent(root_mine, X_ONE)
+    region_mine = joined(region_mine, region_other, send)
+    region_other = sent(region_mine, Z_TWO)
     (back,) = call(
         back_kernel,
         [HBM] * 2,
@@ -363,43 +372,53 @@
         w,
         after(white, total),
     )
-    region_mine = doubled(after(region_mine, back), Y_ONE)
-    root_mine = doubled(after(root_mine, back), X_THREE)
-    root_mine = root_mine.reshape(X * Z_HI, 64, width)
-    (total,) = call(
+    root_mine = joined(root_mine, root_other, back)
+    root_other = sent(root_mine, X_THREE)
+    region_mine = joined(region_mine, region_other, total)
+    region_other = sent(region_mine, Y_ONE)
+    (leaf_total,) = call(
         sum_kernel,
-        [VMEM],
+        [VMEM] * Y,
         [(shaped(Z_LO * Z_HI, 2, 16, width), VMEM)],
         [],
         0,
         8,
-        exchange(total, "leaf", ALONG_Y),
-    )
-    region_mine = doubled(after(region_mine, total), Y_THREE)
-    region_mine = region_mine.reshape(Y * Z_LO, 2, 16, width)
-    root_came = sent(after(root_mine, total), SWAP_CORES)
-    pieces = exchange(total, BOTH, ALONG_Z)
-    root_rows = added(pieces[:, 0]).astype(BF)
-    region_came = sent(after(region_mine, root_rows), SWAP_CORES)
-    others = [sent(root_rows, moves) for moves in (X_ONE, X_THREE, X_TWO)]
-
+        total,
+        *shares,
+    )
+    root_mine = joined(root_mine, root_other, leaf_total).reshape(X * Z_HI, 64, width)
+    root_came = sent(root_mine, SWAP_CORES)
+    region_mine = joined(region_mine, region_other, leaf_total)
+    region_other = sent(region_mine, Y_THREE)
+    pieces = exchange(leaf_total, BOTH, ALONG_Z)
     scale = 1.0 / obs
     factor = VMEM((width, width), BF)
-    grad_root, grad_region, region_part, root_product = call(
-        functools.partial(finish_kernel, scale),
-        [VMEM] * 5 + [HBM],
-        [
-            (shaped(1, obs, width), HBM),
-            (shaped(1, obs, width), HBM),
-            (shaped(1, 16, width, dtype=F32), VMEM),
-            (shaped(width, width), VMEM),
-        ],
-        [factor, factor, factor, square, strip, strip, dma(tiles), dma(2 * tiles)],
-        2 * 2 * obs * width * width + 8 * width**3,
-        20,
+    held = [strip, strip, dma(tiles), dma(tiles)]
+    work = 2 * obs * width * width + 4 * width**3
+    grad_root, root_product = call(
+        root_kernel,
+        [VMEM] * 2 + [HBM],
+        [(shaped(1, obs, width), HBM), (shaped(width, width), VMEM)],
+        [factor, factor, *held],
+        work,
+        16,
         root_mine,
         root_came,
-        region_mine,
+        back,
+    )
+    root_rows = added(after(pieces, root_product)[:, 0]).astype(BF)
+    region_mine = joined(region_mine, region_other).reshape(Y * Z_LO, 2, 16, width)
+    region_came = sent(region_mine, SWAP_CORES)
+    others = [sent(root_rows, moves) for moves in (X_ONE, X_THREE, X_TWO)]
+
+    grad_region, region_part = call(
+        functools.partial(region_kernel, scale),
+        [VMEM] * 3 + [HBM],
+        [(shaped(1, obs, width), HBM), (shaped(1, 16, width, dtype=F32), VMEM)],
+        [factor, factor, factor, *held],
+        work,
+        16,
+        after(region_mine),
         region_came,
         pieces,
         back,
@@ -411,7 +430,7 @@
         [],
         4 * 16 * width * width,
         4,
-        root_rows,
+        after(root_rows, region_part),
         *others,
         root_product,
     )

time: 58.4 us -> 55.5 us (0.950)
  the two profiles are of different devices: /device:TPU:1 before, /device:TPU:2 now
where the time goes in v3:
time: 55.5 us; the launch traced here: 54.9 us
  starting transfers between devices  27.6 us (50%)
  Pallas kernels  18.5 us (33%)
  waiting for transfers between devices  7.81 us (14%)
  between operations  0.81 us (1%)
    ppermute x16, starting transfers between devices, sent(): return lax.ppermute(x, BOTH, moves)  23.3 us
    pallas_call x8, Pallas kernels, call(): pl.pallas_call(kernel, out_shape=[s if s.dtype == F32 else m(s.shape, s.d...  18.5 us
    all_to_all x1, waiting for transfers between devices, exchange(): lax.all_to_all(pieces, axis, 0, 0, tiled=True, axis_index_groups=groups)  4.39 us
    all_to_all x1, starting transfers between devices, exchange(): lax.all_to_all(pieces, axis, 0, 0, tiled=True, axis_index_groups=groups)  4.27 us
    ppermute x16, waiting for transfers between devices, sent(): return lax.ppermute(x, BOTH, moves)  3.42 us
  transfers between devices with their start and end apart: 17, of which 5 were waited for; matrix products, arithmetic and copies ran while one was open for 0% of the time, Pallas kernels for 31%

profile of v3, /device:TPU:2, one launch (start us, length us, event | category | flops | bytes accessed | tf_op | source)
XLA Modules:
  0.0 54.9 jit_solution(3001933080627971815)
XLA Ops:
  0.6 0.9 %shard_map.102 = (bf16[64,512]{1,0:T(8,128)(2,1)S(1)}, bf16[2,16,512]{2,1,0:T(8,128)(2,1)S(1)}) custom-call(bf16[64,512]{1,0:T(8,128)(2,1)} %root_f.1, bf16[64,512]{1,0:T(8,128)(2,1)} %root_a.1, bf16[1,16,512]{2,1,0:T(8,128)(2,1)} %region_f.1, bf16[1,16,512]{2,1,0:T(8,128)(2,1)} %region_a.1), custom_call_target="tpu_custom_call" | custom-call | flops 1000000 | bytes 1000 | tf_op jit(solution)/shard_map/pallas_call | solution.py:85
  1.5 5.9 %collective-permute-start = (bf16[64,512]{1,0:T(8,128)(2,1)S(1)}, bf16[64,512]{1,0:T(8,128)(2,1)S(1)}, u32[]{:S(2)}, u32[]{:S(2)}) collective-permute-start(bf16[64,512]{1,0:T(8,128)(2,1)S(1)} %get-tuple-element.37), channel_id=1, source_target_pairs={{0,56},{1,57},{2,58},{3,59},{4,60},{5,61},{6,62},{7,63},{8,48},{9,... | collective-permute-start | bytes 196616 | tf_op jit(solution)/shard_map/ppermute | solution.py:58
  7.5 1.9 %collective-permute-start.2 = (bf16[2,16,512]{2,1,0:T(8,128)(2,1)S(1)}, bf16[2,16,512]{2,1,0:T(8,128)(2,1)S(1)}, u32[]{:S(2)}, u32[]{:S(2)}) collective-permute-start(bf16[2,16,512]{2,1,0:T(8,128)(2,1)S(1)} %get-tuple-element.55), channel_id=1, source_target_pairs={{0,8},{1,9},{2,10},{3,11},{4,12},{5,13},{6,14},{7,15},{8,0},{9,1},... | collective-permute-start | bytes 98312 | tf_op jit(solution)/shard_map/ppermute | solution.py:58
  9.4 4.4 %shard_map.103 = (bf16[1024,1024]{1,0:T(8,128)(2,1)}, bf16[4,2,4,16,512]{4,3,2,1,0:T(8,128)(2,1)S(1)}, bf16[4,2,4,16,512]{4,3,2,1,0:T(8,128)(2,1)S(1)}) custom-call(bf16[1024,1024]{1,0:T(8,128)(2,1)} %bitcast.37, bf16[1024,512]{1,0:T(8,128)(2,1)} %bitcast.39, bf16[1024,512]{1,0:T(8,128)(2,1)} %bitcast.40), custom_call_target="tpu_custom_call" | custom-call | flops 3000000000 | bytes 3000000 | tf_op jit(solution)/shard_map/pallas_call | solution.py:85
  13.8 0.1 collective-permute-start.3
  13.9 0.6 %collective-permute-start.9 = (bf16[2,2,16,512]{3,2,1,0:T(8,128)(2,1)S(1)}, bf16[2,2,16,512]{3,2,1,0:T(8,128)(2,1)S(1)}, u32[]{:S(2)}, u32[]{:S(2)}) collective-permute-start(bf16[2,2,16,512]{3,2,1,0:T(8,128)(2,1)S(1)} %pad_maximum_fusion.6), channel_id=1, source_target_pairs={{0,16},{1,17},{2,18},{3,19},{4,20},{5,21},{6,22},{7,23},{8,24},{9,... | collective-permute-start | bytes 196616 | tf_op jit(solution)/shard_map/ppermute | solution.py:58
  14.6 0.6 %collective-permute-start.1 = (bf16[2,64,512]{2,1,0:T(8,128)(2,1)S(1)}, bf16[2,64,512]{2,1,0:T(8,128)(2,1)S(1)}, u32[]{:S(2)}, u32[]{:S(2)}) collective-permute-start(bf16[2,64,512]{2,1,0:T(8,128)(2,1)S(1)} %pad_maximum_fusion.4), channel_id=1, source_target_pairs={{0,64},{1,65},{2,66},{3,67},{4,68},{5,69},{6,70},{7,71},{8,72},{9,... | collective-permute-start | bytes 393224 | tf_op jit(solution)/shard_map/ppermute | solution.py:58
  15.2 0.6 %collective-permute-done.3.came = bf16[4,2,4,16,512]{4,3,2,1,0:T(8,128)(2,1)S(1)} collective-permute-done((bf16[4,2,4,16,512]{4,3,2,1,0:T(8,128)(2,1)S(1)}, bf16[4,2,4,16,512]{4,3,2,1,0:T(8,128)(2,1)S(1)}, u32[]{:S(2)}, u32[]{:S(2)}) %collective-permute-start.3) | collective-permute-done | bytes 524320 | tf_op jit(solution)/shard_map/ppermute | solution.py:58
  15.8 0.1 shard_map.104
  16.0 3.3 %collective-permute-start.5 = (bf16[2,4,16,512]{3,2,1,0:T(8,128)(2,1)S(1)}, bf16[2,4,16,512]{3,2,1,0:T(8,128)(2,1)S(1)}, u32[]{:S(2)}, u32[]{:S(2)}) collective-permute-start(bf16[2,4,16,512]{3,2,1,0:T(8,128)(2,1)S(1)} %get-tuple-element.49), channel_id=1, source_target_pairs={{0,4},{1,5},{2,6},{3,7},{4,0},{5,1},{6,2},{7,3},{8,12},{9,13},{10,... | collective-permute-start | bytes 393224 | tf_op jit(solution)/shard_map/ppermute | solution.py:58
  19.2 0.7 %collective-permute-start.6 = (bf16[2,4,16,512]{3,2,1,0:T(8,128)(2,1)S(1)}, bf16[2,4,16,512]{3,2,1,0:T(8,128)(2,1)S(1)}, u32[]{:S(2)}, u32[]{:S(2)}) collective-permute-start(bf16[2,4,16,512]{3,2,1,0:T(8,128)(2,1)S(1)} %get-tuple-element.50), channel_id=1, source_target_pairs={{0,2},{1,3},{2,0},{3,1},{4,6},{5,7},{6,4},{7,5},{8,10},{9,11},{10,... | collective-permute-start | bytes 393224 | tf_op jit(solution)/shard_map/ppermute | solution.py:58
  19.9 0.4 collective-permute-start.7
  20.3 0.1 collective-permute-done.9
  20.4 1.7 %collective-permute-start.10 = (bf16[2,2,2,16,512]{4,3,2,1,0:T(8,128)(2,1)S(1)}, bf16[2,2,2,16,512]{4,3,2,1,0:T(8,128)(2,1)S(1)}, u32[]{:S(2)}, u32[]{:S(2)}) collective-permute-start(bf16[2,2,2,16,512]{4,3,2,1,0:T(8,128)(2,1)S(1)} %pad_maximum_fusion.5), channel_id=1, source_target_pairs={{0,2},{1,3},{2,0},{3,1},{4,6},{5,7},{6,4},{7,5},{8,10},{9,11},{10,... | collective-permute-start | bytes 393224 | tf_op jit(solution)/shard_map/ppermute | solution.py:58
  22.0 4.3 %shard_map.105.back_hbm = bf16[1024,1024]{1,0:T(8,128)(2,1)} custom-call(bf16[1024,1024]{1,0:T(8,128)(2,1)} %bitcast.38, bf16[1024,1024]{1,0:T(8,128)(2,1)} %get-tuple-element.46.white_hbm), custom_call_target="tpu_custom_call" | custom-call | flops 2000000000 | bytes 2000000 | tf_op jit(solution)/shard_map/pallas_call | solution.py:85
  26.4 1.6 %collective-permute-start.4 = (bf16[2,2,64,512]{3,2,1,0:T(8,128)(2,1)S(1)}, bf16[2,2,64,512]{3,2,1,0:T(8,128)(2,1)S(1)}, u32[]{:S(2)}, u32[]{:S(2)}) collective-permute-start(bf16[2,2,64,512]{3,2,1,0:T(8,128)(2,1)S(1)} %pad_maximum_fusion.2), channel_id=1, source_target_pairs={{0,192},{1,193},{2,194},{3,195},{4,196},{5,197},{6,198},{7,199},{8... | collective-permute-start | bytes 786440 | tf_op jit(solution)/shard_map/ppermute | solution.py:58
  28.0 0.8 %shard_map.106 = bf16[8,2,16,512]{3,2,1,0:T(8,128)(2,1)} custom-call(bf16[2,4,16,512]{3,2,1,0:T(8,128)(2,1)S(1)} %get-tuple-element.45.a, bf16[2,4,16,512]{3,2,1,0:T(8,128)(2,1)S(1)} %collective-permute-done.5.b, bf16[2,4,16,512]{3,2,1,0:T(8,128)(2,1)S(1)} %collective-permute-done.6.c, bf16[2,4,16,512]{3,2,1,0:T(8,128)(2,1)S(1)} %collective-permute-done.7.d), custom_call_target="tpu_custom_call" | custom-call | flops 100000000 | bytes 100000 | tf_op jit(solution)/shard_map/pallas_call | solution.py:85
  28.8 0.3 collective-permute-done.10
  29.1 2.0 %collective-permute-start.11 = (bf16[2,2,2,2,16,512]{5,4,3,2,1,0:T(8,128)(2,1)S(1)}, bf16[2,2,2,2,16,512]{5,4,3,2,1,0:T(8,128)(2,1)S(1)}, u32[]{:S(2)}, u32[]{:S(2)}) collective-permute-start(bf16[2,2,2,2,16,512]{5,4,3,2,1,0:T(8,128)(2,1)S(1)} %pad_maximum_fusion.3), channel_id=1, source_target_pairs={{0,6},{1,7},{2,4},{3,5},{4,2},{5,3},{6,0},{7,1},{8,14},{9,15},{10,... | collective-permute-start | bytes 786440 | tf_op jit(solution)/shard_map/ppermute | solution.py:58
  31.0 4.3 %all-to-all-start = ((bf16[8,2,16,512]{3,2,1,0:T(8,128)(2,1)}), bf16[8,2,16,512]{3,2,1,0:T(8,128)(2,1)S(1)}, u32[]{:S(2)}, u32[]{:S(2)}) async-start(bf16[8,2,16,512]{3,2,1,0:T(8,128)(2,1)} %shard_map.106), calls=%async_computation | async-start | bytes 524288 | tf_op jit(solution)/shard_map/all_to_all | solution.py:54
  35.3 0.1 pad_maximum_fusion
  35.4 0.1 collective-permute-start.8
  35.5 2.4 %collective-permute-done.11 = bf16[2,2,2,2,16,512]{5,4,3,2,1,0:T(8,128)(2,1)S(1)} collective-permute-done((bf16[2,2,2,2,16,512]{5,4,3,2,1,0:T(8,128)(2,1)S(1)}, bf16[2,2,2,2,16,512]{5,4,3,2,1,0:T(8,128)(2,1)S(1)}, u32[]{:S(2)}, u32[]{:S(2)}) %collective-permute-start.11) | collective-permute-done | bytes 262176 | tf_op jit(solution)/shard_map/ppermute | solution.py:58
  37.9 0.1 pad_maximum_fusion.1
  38.0 0.3 collective-permute-start.12
  38.2 3.3 %shard_map.107 = (bf16[1,1024,512]{2,1,0:T(8,128)(2,1)}, bf16[512,512]{1,0:T(8,128)(2,1)S(1)}) custom-call(bf16[8,64,512]{2,1,0:T(8,128)(2,1)S(1)} %bitcast.20, bf16[8,64,512]{2,1,0:T(8,128)(2,1)S(1)} %collective-permute-done.8.came_ref, bf16[1024,1024]{1,0:T(8,128)(2,1)} %shard_map.105.back_hbm), custom_call_target="tpu_custom_call" | custom-call | tf_op jit(solution)/shard_map/pallas_call | solution.py:85
  41.5 4.4 %all-to-all-done.pieces = bf16[8,2,16,512]{3,2,1,0:T(8,128)(2,1)S(1)} async-done(((bf16[8,2,16,512]{3,2,1,0:T(8,128)(2,1)}), bf16[8,2,16,512]{3,2,1,0:T(8,128)(2,1)S(1)}, u32[]{:S(2)}, u32[]{:S(2)}) %all-to-all-start) | async-done | bytes 262176 | tf_op jit(solution)/shard_map/all_to_all | solution.py:54
  46.0 1.9 %collective-permute-start.13 = (bf16[16,512]{1,0:T(8,128)(2,1)S(1)}, bf16[16,512]{1,0:T(8,128)(2,1)S(1)}, u32[]{:S(2)}, u32[]{:S(2)}) collective-permute-start(bf16[16,512]{1,0:T(8,128)(2,1)S(1)} %slice_reduce_fusion.a), channel_id=1, source_target_pairs={{0,64},{1,65},{2,66},{3,67},{4,68},{5,69},{6,70},{7,71},{8,72},{9,... | collective-permute-start | bytes 49160 | tf_op jit(solution)/shard_map/ppermute | solution.py:58
  47.9 0.4 collective-permute-start.14
  48.3 1.8 %collective-permute-start.15 = (bf16[16,512]{1,0:T(8,128)(2,1)S(1)}, bf16[16,512]{1,0:T(8,128)(2,1)S(1)}, u32[]{:S(2)}, u32[]{:S(2)}) collective-permute-start(bf16[16,512]{1,0:T(8,128)(2,1)S(1)} %slice_reduce_fusion.a), channel_id=1, source_target_pairs={{0,128},{1,129},{2,130},{3,131},{4,132},{5,133},{6,134},{7,135},{8... | collective-permute-start | bytes 49160 | tf_op jit(solution)/shard_map/ppermute | solution.py:58
  50.1 3.9 %shard_map.108 = (bf16[1,1024,512]{2,1,0:T(8,128)(2,1)}, f32[1,16,512]{2,1,0:T(8,128)}) custom-call(bf16[16,2,16,512]{3,2,1,0:T(8,128)(2,1)S(1)} %bitcast.22, bf16[16,2,16,512]{3,2,1,0:T(8,128)(2,1)S(1)} %collective-permute-done.12.came_ref, bf16[8,2,16,512]{3,2,1,0:T(8,128)(2,1)S(1)} %all-to-all-done.pieces, bf16[1024,1024]{1,0:T(8,128)(2,1)} %shard_map.105.back_hbm), custom_call_target="tpu_custom_call" | custom-call | flops 1500000000 | bytes 1500000 | tf_op jit(solution)/shard_map/pallas_call | solution.py:85
  54.1 0.8 %shard_map.109 = f32[16,512]{1,0:T(8,128)} custom-call(bf16[16,512]{1,0:T(8,128)(2,1)S(1)} %slice_reduce_fusion.a, bf16[16,512]{1,0:T(8,128)(2,1)S(1)} %collective-permute-done.13.b, bf16[16,512]{1,0:T(8,128)(2,1)S(1)} %collective-permute-done.14.c, bf16[16,512]{1,0:T(8,128)(2,1)S(1)} %collective-permute-done.15.d, bf16[512,512]{1,0:T(8,128)(2,1)S(1)} %get-tuple-element.64.factor), custom_call_target="tpu_custom_call" | custom-call | flops 30000000 | bytes 30000 | tf_op jit(solution)/shard_map/pallas_call | solution.py:85
  (18 shorter events, 0.1 us)
Async XLA Ops:
  1.5 12.3 %collective-permute-start = (bf16[64,512]{1,0:T(8,128)(2,1)S(1)}, bf16[64,512]{1,0:T(8,128)(2,1)S(1)}, u32[]{:S(2)}, u32[]{:S(2)}) collective-permute-start(bf16[64,512]{1,0:T(8,128)(2,1)S(1)} %get-tuple-element.37), channel_id=1, source_target_pairs={{0,56},{1,57},{2,58},{3,59},{4,60},{5,61},{6,62},{7,63},{8,48},{9,... | collective-permute-start | bytes 196616 | tf_op jit(solution)/shard_map/ppermute | solution.py:58
  7.5 6.3 %collective-permute-start.2 = (bf16[2,16,512]{2,1,0:T(8,128)(2,1)S(1)}, bf16[2,16,512]{2,1,0:T(8,128)(2,1)S(1)}, u32[]{:S(2)}, u32[]{:S(2)}) collective-permute-start(bf16[2,16,512]{2,1,0:T(8,128)(2,1)S(1)} %get-tuple-element.55), channel_id=1, source_target_pairs={{0,8},{1,9},{2,10},{3,11},{4,12},{5,13},{6,14},{7,15},{8,0},{9,1},... | collective-permute-start | bytes 98312 | tf_op jit(solution)/shard_map/ppermute | solution.py:58
  13.8 2.0 %collective-permute-start.3 = (bf16[4,2,4,16,512]{4,3,2,1,0:T(8,128)(2,1)S(1)}, bf16[4,2,4,16,512]{4,3,2,1,0:T(8,128)(2,1)S(1)}, u32[]{:S(2)}, u32[]{:S(2)}) collective-permute-start(bf16[4,2,4,16,512]{4,3,2,1,0:T(8,128)(2,1)S(1)} %get-tuple-element.44), channel_id=1, source_target_pairs={{0,1},{1,0},{2,3},{3,2},{4,5},{5,4},{6,7},{7,6},{8,9},{9,8},{10,11... | collective-permute-start | bytes 1572872 | tf_op jit(solution)/shard_map/ppermute | solution.py:58
  13.9 6.4 %collective-permute-start.9 = (bf16[2,2,16,512]{3,2,1,0:T(8,128)(2,1)S(1)}, bf16[2,2,16,512]{3,2,1,0:T(8,128)(2,1)S(1)}, u32[]{:S(2)}, u32[]{:S(2)}) collective-permute-start(bf16[2,2,16,512]{3,2,1,0:T(8,128)(2,1)S(1)} %pad_maximum_fusion.6), channel_id=1, source_target_pairs={{0,16},{1,17},{2,18},{3,19},{4,20},{5,21},{6,22},{7,23},{8,24},{9,... | collective-permute-start | bytes 196616 | tf_op jit(solution)/shard_map/ppermute | solution.py:58
  14.6 11.8 %collective-permute-start.1 = (bf16[2,64,512]{2,1,0:T(8,128)(2,1)S(1)}, bf16[2,64,512]{2,1,0:T(8,128)(2,1)S(1)}, u32[]{:S(2)}, u32[]{:S(2)}) collective-permute-start(bf16[2,64,512]{2,1,0:T(8,128)(2,1)S(1)} %pad_maximum_fusion.4), channel_id=1, source_target_pairs={{0,64},{1,65},{2,66},{3,67},{4,68},{5,69},{6,70},{7,71},{8,72},{9,... | collective-permute-start | bytes 393224 | tf_op jit(solution)/shard_map/ppermute | solution.py:58
  16.0 12.0 %collective-permute-start.5 = (bf16[2,4,16,512]{3,2,1,0:T(8,128)(2,1)S(1)}, bf16[2,4,16,512]{3,2,1,0:T(8,128)(2,1)S(1)}, u32[]{:S(2)}, u32[]{:S(2)}) collective-permute-start(bf16[2,4,16,512]{3,2,1,0:T(8,128)(2,1)S(1)} %get-tuple-element.49), channel_id=1, source_target_pairs={{0,4},{1,5},{2,6},{3,7},{4,0},{5,1},{6,2},{7,3},{8,12},{9,13},{10,... | collective-permute-start | bytes 393224 | tf_op jit(solution)/shard_map/ppermute | solution.py:58
  19.2 8.7 %collective-permute-start.6 = (bf16[2,4,16,512]{3,2,1,0:T(8,128)(2,1)S(1)}, bf16[2,4,16,512]{3,2,1,0:T(8,128)(2,1)S(1)}, u32[]{:S(2)}, u32[]{:S(2)}) collective-permute-start(bf16[2,4,16,512]{3,2,1,0:T(8,128)(2,1)S(1)} %get-tuple-element.50), channel_id=1, source_target_pairs={{0,2},{1,3},{2,0},{3,1},{4,6},{5,7},{6,4},{7,5},{8,10},{9,11},{10,... | collective-permute-start | bytes 393224 | tf_op jit(solution)/shard_map/ppermute | solution.py:58
  19.9 8.1 %collective-permute-start.7 = (bf16[2,4,16,512]{3,2,1,0:T(8,128)(2,1)S(1)}, bf16[2,4,16,512]{3,2,1,0:T(8,128)(2,1)S(1)}, u32[]{:S(2)}, u32[]{:S(2)}) collective-permute-start(bf16[2,4,16,512]{3,2,1,0:T(8,128)(2,1)S(1)} %get-tuple-element.51), channel_id=1, source_target_pairs={{0,6},{1,7},{2,4},{3,5},{4,2},{5,3},{6,0},{7,1},{8,14},{9,15},{10,... | collective-permute-start | bytes 393224 | tf_op jit(solution)/shard_map/ppermute | solution.py:58
  20.4 8.7 %collective-permute-start.10 = (bf16[2,2,2,16,512]{4,3,2,1,0:T(8,128)(2,1)S(1)}, bf16[2,2,2,16,512]{4,3,2,1,0:T(8,128)(2,1)S(1)}, u32[]{:S(2)}, u32[]{:S(2)}) collective-permute-start(bf16[2,2,2,16,512]{4,3,2,1,0:T(8,128)(2,1)S(1)} %pad_maximum_fusion.5), channel_id=1, source_target_pairs={{0,2},{1,3},{2,0},{3,1},{4,6},{5,7},{6,4},{7,5},{8,10},{9,11},{10,... | collective-permute-start | bytes 393224 | tf_op jit(solution)/shard_map/ppermute | solution.py:58
  26.4 8.9 %collective-permute-start.4 = (bf16[2,2,64,512]{3,2,1,0:T(8,128)(2,1)S(1)}, bf16[2,2,64,512]{3,2,1,0:T(8,128)(2,1)S(1)}, u32[]{:S(2)}, u32[]{:S(2)}) collective-permute-start(bf16[2,2,64,512]{3,2,1,0:T(8,128)(2,1)S(1)} %pad_maximum_fusion.2), channel_id=1, source_target_pairs={{0,192},{1,193},{2,194},{3,195},{4,196},{5,197},{6,198},{7,199},{8... | collective-permute-start | bytes 786440 | tf_op jit(solution)/shard_map/ppermute | solution.py:58
  29.1 8.8 %collective-permute-start.11 = (bf16[2,2,2,2,16,512]{5,4,3,2,1,0:T(8,128)(2,1)S(1)}, bf16[2,2,2,2,16,512]{5,4,3,2,1,0:T(8,128)(2,1)S(1)}, u32[]{:S(2)}, u32[]{:S(2)}) collective-permute-start(bf16[2,2,2,2,16,512]{5,4,3,2,1,0:T(8,128)(2,1)S(1)} %pad_maximum_fusion.3), channel_id=1, source_target_pairs={{0,6},{1,7},{2,4},{3,5},{4,2},{5,3},{6,0},{7,1},{8,14},{9,15},{10,... | collective-permute-start | bytes 786440 | tf_op jit(solution)/shard_map/ppermute | solution.py:58
  31.0 14.9 %all-to-all-start = ((bf16[8,2,16,512]{3,2,1,0:T(8,128)(2,1)}), bf16[8,2,16,512]{3,2,1,0:T(8,128)(2,1)S(1)}, u32[]{:S(2)}, u32[]{:S(2)}) async-start(bf16[8,2,16,512]{3,2,1,0:T(8,128)(2,1)} %shard_map.106), calls=%async_computation | async-start | bytes 524288 | tf_op jit(solution)/shard_map/all_to_all | solution.py:54
  35.4 2.9 %collective-permute-start.8 = (bf16[8,64,512]{2,1,0:T(8,128)(2,1)S(1)}, bf16[8,64,512]{2,1,0:T(8,128)(2,1)S(1)}, u32[]{:S(2)}, u32[]{:S(2)}) collective-permute-start(bf16[8,64,512]{2,1,0:T(8,128)(2,1)S(1)} %bitcast.19), channel_id=1, source_target_pairs={{0,1},{1,0},{2,3},{3,2},{4,5},{5,4},{6,7},{7,6},{8,9},{9,8},{10,11... | collective-permute-start | bytes 1572872 | tf_op jit(solution)/shard_map/ppermute | solution.py:58
  38.0 12.2 %collective-permute-start.12 = (bf16[16,2,16,512]{3,2,1,0:T(8,128)(2,1)S(1)}, bf16[16,2,16,512]{3,2,1,0:T(8,128)(2,1)S(1)}, u32[]{:S(2)}, u32[]{:S(2)}) collective-permute-start(bf16[16,2,16,512]{3,2,1,0:T(8,128)(2,1)S(1)} %bitcast.21), channel_id=1, source_target_pairs={{0,1},{1,0},{2,3},{3,2},{4,5},{5,4},{6,7},{7,6},{8,9},{9,8},{10,11... | collective-permute-start | bytes 1572872 | tf_op jit(solution)/shard_map/ppermute | solution.py:58
  46.0 8.1 %collective-permute-start.13 = (bf16[16,512]{1,0:T(8,128)(2,1)S(1)}, bf16[16,512]{1,0:T(8,128)(2,1)S(1)}, u32[]{:S(2)}, u32[]{:S(2)}) collective-permute-start(bf16[16,512]{1,0:T(8,128)(2,1)S(1)} %slice_reduce_fusion.a), channel_id=1, source_target_pairs={{0,64},{1,65},{2,66},{3,67},{4,68},{5,69},{6,70},{7,71},{8,72},{9,... | collective-permute-start | bytes 49160 | tf_op jit(solution)/shard_map/ppermute | solution.py:58
  47.9 6.2 %collective-permute-start.14 = (bf16[16,512]{1,0:T(8,128)(2,1)S(1)}, bf16[16,512]{1,0:T(8,128)(2,1)S(1)}, u32[]{:S(2)}, u32[]{:S(2)}) collective-permute-start(bf16[16,512]{1,0:T(8,128)(2,1)S(1)} %slice_reduce_fusion.a), channel_id=1, source_target_pairs={{0,192},{1,193},{2,194},{3,195},{4,196},{5,197},{6,198},{7,199},{8... | collective-permute-start | bytes 49160 | tf_op jit(solution)/shard_map/ppermute | solution.py:58
  48.3 5.8 %collective-permute-start.15 = (bf16[16,512]{1,0:T(8,128)(2,1)S(1)}, bf16[16,512]{1,0:T(8,128)(2,1)S(1)}, u32[]{:S(2)}, u32[]{:S(2)}) collective-permute-start(bf16[16,512]{1,0:T(8,128)(2,1)S(1)} %slice_reduce_fusion.a), channel_id=1, source_target_pairs={{0,128},{1,129},{2,130},{3,131},{4,132},{5,133},{6,134},{7,135},{8... | collective-permute-start | bytes 49160 | tf_op jit(solution)/shard_map/ppermute | solution.py:58

commit v4 on v3

--- a/solution.py
+++ b/solution.py
@@ -180,11 +180,10 @@
         copy.wait()
 
 
-def back_kernel(w_hbm, white_hbm, out_hbm, w, white, out, in_sem, out_sem):
+def back_kernel(w_hbm, white_hbm, out, w, white, in_sem):
     n = w_hbm.shape[0]
-    width = white.shape[1] // 2
     tiles = n // TILE
-    arrivals, leaving = [], []
+    arrivals = []
     for i in reversed(range(tiles)):
         rows, k = pl.ds(TILE * i, TILE), pl.ds(0, TILE * (i + 1))
         pair = [
@@ -198,16 +197,8 @@
         for copy in pair:
             copy.wait()
         rows = slice(TILE * i, TILE * (i + 1))
-        for level in range(2):
-            cols = slice(level * width, (level + 1) * width)
-            out[rows, cols] = dot(
-                w[TILE * i :, rows], white[TILE * i :, cols], ((0,), (0,))
-            ).astype(BF)
-        rows = pl.ds(TILE * i, TILE)
-        leaving.append(pltpu.make_async_copy(out.at[rows], out_hbm.at[rows], out_sem.at[i]))
-        leaving[-1].start()
-    for copy in leaving:
-        copy.wait()
+        product = dot(w[TILE * i :, rows], white[TILE * i :, :], ((0,), (0,)))
+        out[rows, :] = product.astype(BF)
 
 
 def merge_kernel(own, came, *outs):
@@ -233,23 +224,13 @@
     return (out[:16] + out[16:]) * scale
 
 
-def start_back(level, back_hbm, back, in_sem):
-    width = back.shape[1]
-    copies = []
-    for i in range(back.shape[0] // TILE):
+def gradients(level, back, product, part, out, out_sem):
+    width = part.shape[1]
+    leaving = []
+    for i in range(part.shape[0] // TILE):
         rows = pl.ds(TILE * i, TILE)
-        source = back_hbm.at[rows, pl.ds(level * width, width)]
-        copies.append(pltpu.make_async_copy(source, back.at[rows], in_sem.at[i]))
-        copies[-1].start()
-    return copies
-
-
-def gradients(arrivals, back, product, part, out, out_sem):
-    leaving = []
-    for i, copy in enumerate(arrivals):
-        copy.wait()
-        rows = pl.ds(TILE * i, TILE)
-        part[rows, :] = dot(back[rows, :], product[...]).astype(BF)
+        cols = slice(level * width, (level + 1) * width)
+        part[rows, :] = dot(back[rows, cols], product[...]).astype(BF)
         leaving.append(pltpu.make_async_copy(part.at[rows], out.at[0, rows], out_sem.at[i]))
         leaving[-1].start()
     for copy in leaving:
@@ -261,10 +242,9 @@
     return product.astype(BF)
 
 
-def root_kernel(mine_ref, came_ref, back_hbm, out_hbm, product, f, a, back, part, in_sem, out_sem):
+def root_kernel(mine_ref, came_ref, back, out_hbm, product, f, a, part, out_sem):
     x, _, hi, _, core = position()
     first = core == 0
-    arrivals = start_back(0, back_hbm, back, in_sem)
     for j in range(X * Z_HI):
         rows = slice(64 * j, 64 * (j + 1))
         v = x ^ (j // Z_HI)
@@ -274,7 +254,7 @@
         f[rows, :] = jnp.where(first, mine, came)
         a[rows, :] = jnp.where(first, came, mine)
     product[...] = factor_product(f, a)
-    gradients(arrivals, back, product, part, out_hbm, out_sem)
+    gradients(0, back, product, part, out_hbm, out_sem)
 
 
 def region_kernel(
@@ -282,20 +262,17 @@
     mine_ref,
     came_ref,
     pieces,
-    back_hbm,
+    back,
     out_hbm,
     rows_out,
     f,
     a,
     product,
-    back,
     part,
-    in_sem,
     out_sem,
 ):
     _, y, hi, lo, core = position()
     first = core == 0
-    arrivals = start_back(1, back_hbm, back, in_sem)
     for j in range(Z_LO * Y):
         v = y ^ (j % Y)
         t = v >> 1
@@ -309,7 +286,7 @@
     for k in range(1, Z_LO):
         total = total + pieces[hi * Z_LO + k, 1].astype(F32)
     rows_out[0] = product_of_rows(total, product[...], scale)
-    gradients(arrivals, back, product, part, out_hbm, out_sem)
+    gradients(1, back, product, part, out_hbm, out_sem)
 
 
 def root_rows_kernel(scale, a, b, c, d, factor, out_ref):
@@ -365,8 +342,8 @@
     (back,) = call(
         back_kernel,
         [HBM] * 2,
-        [(shaped(obs, 2 * width), HBM)],
-        [VMEM((obs, obs), BF), square, square, dma(2 * tiles), dma(tiles)],
+        [(shaped(obs, 2 * width), VMEM)],
+        [VMEM((obs, obs), BF), square, dma(2 * tiles)],
         2 * 2 * obs * obs * width,
         20,
         w,
@@ -393,11 +370,11 @@
     pieces = exchange(leaf_total, BOTH, ALONG_Z)
     scale = 1.0 / obs
     factor = VMEM((width, width), BF)
-    held = [strip, strip, dma(tiles), dma(tiles)]
+    held = [strip, dma(tiles)]
     work = 2 * obs * width * width + 4 * width**3
     grad_root, root_product = call(
         root_kernel,
-        [VMEM] * 2 + [HBM],
+        [VMEM] * 3,
         [(shaped(1, obs, width), HBM), (shaped(width, width), VMEM)],
         [factor, factor, *held],
         work,
@@ -413,7 +390,7 @@
 
     grad_region, region_part = call(
         functools.partial(region_kernel, scale),
-        [VMEM] * 3 + [HBM],
+        [VMEM] * 4,
         [(shaped(1, obs, width), HBM), (shaped(1, 16, width, dtype=F32), VMEM)],
         [factor, factor, factor, *held],
         work,

time: 55.5 us -> 55.1 us (level)
  Pallas kernels: 18.5 us -> 16.5 us
  waiting for transfers between devices: 7.81 us -> 9.2 us
  other arithmetic: 0.21 us -> 1.16 us
  starting transfers between devices: 27.6 us -> 26.7 us
    ppermute x16, waiting for transfers between devices: 3.42 us -> 5.44 us  [sent(): return lax.ppermute(x, BOTH, moves)]
    pallas_call x8, Pallas kernels: 18.5 us -> 16.5 us  [call(): pl.pallas_call(kernel, out_shape=[s if s.dtype == F32 else m(s.shape, s.d...]
    another operation x7, other arithmetic: 0.19 us -> 1.14 us  [joined(): return jnp.stack(lax.optimization_barrier((x, came, *behind))[:2])]
    ppermute x16, starting transfers between devices: 23.3 us -> 22.5 us  [sent(): return lax.ppermute(x, BOTH, moves)]
    all_to_all x1, waiting for transfers between devices: 4.39 us -> 3.76 us  [exchange(): lax.all_to_all(pieces, axis, 0, 0, tiled=True, axis_index_groups=groups)]
  transfers between devices with their start and end apart: 17 -> 17, of which waited for: 5 -> 6; matrix products, arithmetic and copies ran while one was open for 0% -> 2% of each run, Pallas kernels for 31% -> 27%
where the time goes in v4:
time: 55.1 us; the launch traced here: 54.4 us
  starting transfers between devices  26.7 us (48%)
  Pallas kernels  16.5 us (30%)
  waiting for transfers between devices  9.2 us (17%)
  other arithmetic  1.16 us (2%)
  between operations  0.8 us (1%)
    ppermute x16, starting transfers between devices, sent(): return lax.ppermute(x, BOTH, moves)  22.5 us
    pallas_call x8, Pallas kernels, call(): pl.pallas_call(kernel, out_shape=[s if s.dtype == F32 else m(s.shape, s.d...  16.5 us
    ppermute x16, waiting for transfers between devices, sent(): return lax.ppermute(x, BOTH, moves)  5.44 us
    all_to_all x1, starting transfers between devices, exchange(): lax.all_to_all(pieces, axis, 0, 0, tiled=True, axis_index_groups=groups)  4.27 us
    all_to_all x1, waiting for transfers between devices, exchange(): lax.all_to_all(pieces, axis, 0, 0, tiled=True, axis_index_groups=groups)  3.76 us
    another operation x7, other arithmetic, joined(): return jnp.stack(lax.optimization_barrier((x, came, *behind))[:2])  1.14 us
  transfers between devices with their start and end apart: 17, of which 6 were waited for; matrix products, arithmetic and copies ran while one was open for 2% of the time, Pallas kernels for 27%

profile of v4, /device:TPU:2, one launch (start us, length us, event | category | flops | bytes accessed | tf_op | source)
XLA Modules:
  0.0 54.4 jit_solution(26734767233587975)
XLA Ops:
  0.6 0.9 %shard_map.102 = (bf16[64,512]{1,0:T(8,128)(2,1)S(1)}, bf16[2,16,512]{2,1,0:T(8,128)(2,1)S(1)}) custom-call(bf16[64,512]{1,0:T(8,128)(2,1)} %root_f.1, bf16[64,512]{1,0:T(8,128)(2,1)} %root_a.1, bf16[1,16,512]{2,1,0:T(8,128)(2,1)} %region_f.1, bf16[1,16,512]{2,1,0:T(8,128)(2,1)} %region_a.1), custom_call_target="tpu_custom_call" | custom-call | flops 1000000 | bytes 1000 | tf_op jit(solution)/shard_map/pallas_call | solution.py:85
  1.5 5.9 %collective-permute-start = (bf16[64,512]{1,0:T(8,128)(2,1)S(1)}, bf16[64,512]{1,0:T(8,128)(2,1)S(1)}, u32[]{:S(2)}, u32[]{:S(2)}) collective-permute-start(bf16[64,512]{1,0:T(8,128)(2,1)S(1)} %get-tuple-element.37), channel_id=1, source_target_pairs={{0,56},{1,57},{2,58},{3,59},{4,60},{5,61},{6,62},{7,63},{8,48},{9,... | collective-permute-start | bytes 196616 | tf_op jit(solution)/shard_map/ppermute | solution.py:58
  7.5 1.9 %collective-permute-start.2 = (bf16[2,16,512]{2,1,0:T(8,128)(2,1)S(1)}, bf16[2,16,512]{2,1,0:T(8,128)(2,1)S(1)}, u32[]{:S(2)}, u32[]{:S(2)}) collective-permute-start(bf16[2,16,512]{2,1,0:T(8,128)(2,1)S(1)} %get-tuple-element.55), channel_id=1, source_target_pairs={{0,8},{1,9},{2,10},{3,11},{4,12},{5,13},{6,14},{7,15},{8,0},{9,1},... | collective-permute-start | bytes 98312 | tf_op jit(solution)/shard_map/ppermute | solution.py:58
  9.4 4.4 %shard_map.103 = (bf16[1024,1024]{1,0:T(8,128)(2,1)}, bf16[4,2,4,16,512]{4,3,2,1,0:T(8,128)(2,1)S(1)}, bf16[4,2,4,16,512]{4,3,2,1,0:T(8,128)(2,1)S(1)}) custom-call(bf16[1024,1024]{1,0:T(8,128)(2,1)} %bitcast.36, bf16[1024,512]{1,0:T(8,128)(2,1)} %bitcast.38, bf16[1024,512]{1,0:T(8,128)(2,1)} %bitcast.39), custom_call_target="tpu_custom_call" | custom-call | flops 3000000000 | bytes 3000000 | tf_op jit(solution)/shard_map/pallas_call | solution.py:85
  13.8 0.1 collective-permute-start.3
  13.9 0.6 %collective-permute-start.9 = (bf16[2,2,16,512]{3,2,1,0:T(8,128)(2,1)S(1)}, bf16[2,2,16,512]{3,2,1,0:T(8,128)(2,1)S(1)}, u32[]{:S(2)}, u32[]{:S(2)}) collective-permute-start(bf16[2,2,16,512]{3,2,1,0:T(8,128)(2,1)S(1)} %pad_maximum_fusion.6), channel_id=1, source_target_pairs={{0,16},{1,17},{2,18},{3,19},{4,20},{5,21},{6,22},{7,23},{8,24},{9,... | collective-permute-start | bytes 196616 | tf_op jit(solution)/shard_map/ppermute | solution.py:58
  14.6 0.6 %collective-permute-start.1 = (bf16[2,64,512]{2,1,0:T(8,128)(2,1)S(1)}, bf16[2,64,512]{2,1,0:T(8,128)(2,1)S(1)}, u32[]{:S(2)}, u32[]{:S(2)}) collective-permute-start(bf16[2,64,512]{2,1,0:T(8,128)(2,1)S(1)} %pad_maximum_fusion.4), channel_id=1, source_target_pairs={{0,64},{1,65},{2,66},{3,67},{4,68},{5,69},{6,70},{7,71},{8,72},{9,... | collective-permute-start | bytes 393224 | tf_op jit(solution)/shard_map/ppermute | solution.py:58
  15.2 0.6 %collective-permute-done.3.came = bf16[4,2,4,16,512]{4,3,2,1,0:T(8,128)(2,1)S(1)} collective-permute-done((bf16[4,2,4,16,512]{4,3,2,1,0:T(8,128)(2,1)S(1)}, bf16[4,2,4,16,512]{4,3,2,1,0:T(8,128)(2,1)S(1)}, u32[]{:S(2)}, u32[]{:S(2)}) %collective-permute-start.3) | collective-permute-done | bytes 524320 | tf_op jit(solution)/shard_map/ppermute | solution.py:58
  15.8 0.1 shard_map.104
  16.0 3.3 %collective-permute-start.5 = (bf16[2,4,16,512]{3,2,1,0:T(8,128)(2,1)S(1)}, bf16[2,4,16,512]{3,2,1,0:T(8,128)(2,1)S(1)}, u32[]{:S(2)}, u32[]{:S(2)}) collective-permute-start(bf16[2,4,16,512]{3,2,1,0:T(8,128)(2,1)S(1)} %get-tuple-element.49), channel_id=1, source_target_pairs={{0,4},{1,5},{2,6},{3,7},{4,0},{5,1},{6,2},{7,3},{8,12},{9,13},{10,... | collective-permute-start | bytes 393224 | tf_op jit(solution)/shard_map/ppermute | solution.py:58
  19.2 0.7 %collective-permute-start.6 = (bf16[2,4,16,512]{3,2,1,0:T(8,128)(2,1)S(1)}, bf16[2,4,16,512]{3,2,1,0:T(8,128)(2,1)S(1)}, u32[]{:S(2)}, u32[]{:S(2)}) collective-permute-start(bf16[2,4,16,512]{3,2,1,0:T(8,128)(2,1)S(1)} %get-tuple-element.50), channel_id=1, source_target_pairs={{0,2},{1,3},{2,0},{3,1},{4,6},{5,7},{6,4},{7,5},{8,10},{9,11},{10,... | collective-permute-start | bytes 393224 | tf_op jit(solution)/shard_map/ppermute | solution.py:58
  19.9 0.4 collective-permute-start.7
  20.3 0.1 collective-permute-done.9
  20.4 1.7 %collective-permute-start.10 = (bf16[2,2,2,16,512]{4,3,2,1,0:T(8,128)(2,1)S(1)}, bf16[2,2,2,16,512]{4,3,2,1,0:T(8,128)(2,1)S(1)}, u32[]{:S(2)}, u32[]{:S(2)}) collective-permute-start(bf16[2,2,2,16,512]{4,3,2,1,0:T(8,128)(2,1)S(1)} %pad_maximum_fusion.5), channel_id=1, source_target_pairs={{0,2},{1,3},{2,0},{3,1},{4,6},{5,7},{6,4},{7,5},{8,10},{9,11},{10,... | collective-permute-start | bytes 393224 | tf_op jit(solution)/shard_map/ppermute | solution.py:58
  22.0 3.4 %shard_map.105.back = bf16[1024,1024]{1,0:T(8,128)(2,1)S(1)} custom-call(bf16[1024,1024]{1,0:T(8,128)(2,1)} %bitcast.37, bf16[1024,1024]{1,0:T(8,128)(2,1)} %get-tuple-element.46.white_hbm), custom_call_target="tpu_custom_call" | custom-call | flops 2000000000 | bytes 2000000 | tf_op jit(solution)/shard_map/pallas_call | solution.py:85
  25.5 1.6 %collective-permute-start.4 = (bf16[2,2,64,512]{3,2,1,0:T(8,128)(2,1)S(1)}, bf16[2,2,64,512]{3,2,1,0:T(8,128)(2,1)S(1)}, u32[]{:S(2)}, u32[]{:S(2)}) collective-permute-start(bf16[2,2,64,512]{3,2,1,0:T(8,128)(2,1)S(1)} %pad_maximum_fusion.2), channel_id=1, source_target_pairs={{0,192},{1,193},{2,194},{3,195},{4,196},{5,197},{6,198},{7,199},{8... | collective-permute-start | bytes 786440 | tf_op jit(solution)/shard_map/ppermute | solution.py:58
  27.1 0.8 %shard_map.106 = bf16[8,2,16,512]{3,2,1,0:T(8,128)(2,1)} custom-call(bf16[2,4,16,512]{3,2,1,0:T(8,128)(2,1)S(1)} %get-tuple-element.45.a, bf16[2,4,16,512]{3,2,1,0:T(8,128)(2,1)S(1)} %collective-permute-done.5.b, bf16[2,4,16,512]{3,2,1,0:T(8,128)(2,1)S(1)} %collective-permute-done.6.c, bf16[2,4,16,512]{3,2,1,0:T(8,128)(2,1)S(1)} %collective-permute-done.7.d), custom_call_target="tpu_custom_call" | custom-call | flops 100000000 | bytes 100000 | tf_op jit(solution)/shard_map/pallas_call | solution.py:85
  27.9 1.2 %collective-permute-done.10 = bf16[2,2,2,16,512]{4,3,2,1,0:T(8,128)(2,1)S(1)} collective-permute-done((bf16[2,2,2,16,512]{4,3,2,1,0:T(8,128)(2,1)S(1)}, bf16[2,2,2,16,512]{4,3,2,1,0:T(8,128)(2,1)S(1)}, u32[]{:S(2)}, u32[]{:S(2)}) %collective-permute-start.10) | collective-permute-done | bytes 131104 | tf_op jit(solution)/shard_map/ppermute | solution.py:58
  29.1 1.1 %collective-permute-start.11 = (bf16[2,2,2,2,16,512]{5,4,3,2,1,0:T(8,128)(2,1)S(1)}, bf16[2,2,2,2,16,512]{5,4,3,2,1,0:T(8,128)(2,1)}, u32[]{:S(2)}, u32[]{:S(2)}) collective-permute-start(bf16[2,2,2,2,16,512]{5,4,3,2,1,0:T(8,128)(2,1)S(1)} %pad_maximum_fusion.3), channel_id=1, source_target_pairs={{0,6},{1,7},{2,4},{3,5},{4,2},{5,3},{6,0},{7,1},{8,14},{9,15},{10,... | collective-permute-start | bytes 786440 | tf_op jit(solution)/shard_map/ppermute | solution.py:58
  30.2 4.3 %all-to-all-start = ((bf16[8,2,16,512]{3,2,1,0:T(8,128)(2,1)}), bf16[8,2,16,512]{3,2,1,0:T(8,128)(2,1)S(1)}, u32[]{:S(2)}, u32[]{:S(2)}) async-start(bf16[8,2,16,512]{3,2,1,0:T(8,128)(2,1)} %shard_map.106), calls=%async_computation | async-start | bytes 524288 | tf_op jit(solution)/shard_map/all_to_all | solution.py:54
  34.5 0.1 collective-permute-start.8
  34.6 3.4 %collective-permute-done.11 = bf16[2,2,2,2,16,512]{5,4,3,2,1,0:T(8,128)(2,1)} collective-permute-done((bf16[2,2,2,2,16,512]{5,4,3,2,1,0:T(8,128)(2,1)S(1)}, bf16[2,2,2,2,16,512]{5,4,3,2,1,0:T(8,128)(2,1)}, u32[]{:S(2)}, u32[]{:S(2)}) %collective-permute-start.11) | collective-permute-done | bytes 262176 | tf_op jit(solution)/shard_map/ppermute | solution.py:58
  38.0 1.0 %pad_maximum_fusion.1 = bf16[2,2,2,2,2,16,512]{6,5,4,3,2,1,0:T(8,128)(2,1)S(1)} fusion(bf16[1,2,2,2,2,16,512]{6,5,4,3,2,1,0:T(8,128)(2,1)} %bitcast.17, bf16[1,2,2,2,2,16,512]{6,5,4,3,2,1,0:T(8,128)(2,1)S(1)} %bitcast.26), kind=kLoop, calls=%fused_computation.1 | loop fusion | flops 262144 | bytes 1048576 | tf_op jit(solution)/shard_map/stack | solution.py:66
  39.0 0.3 collective-permute-start.12
  39.3 2.1 %shard_map.107 = (bf16[1,1024,512]{2,1,0:T(8,128)(2,1)}, bf16[512,512]{1,0:T(8,128)(2,1)S(1)}) custom-call(bf16[8,64,512]{2,1,0:T(8,128)(2,1)S(1)} %bitcast.20, bf16[8,64,512]{2,1,0:T(8,128)(2,1)S(1)} %collective-permute-done.8.came_ref, bf16[1024,1024]{1,0:T(8,128)(2,1)S(1)} %shard_map.105.back), custom_call_target="tpu_custom_call" | custom-call | tf_op jit(solution)/shard_map/pallas_call | solution.py:85
  41.4 3.8 %all-to-all-done.pieces = bf16[8,2,16,512]{3,2,1,0:T(8,128)(2,1)S(1)} async-done(((bf16[8,2,16,512]{3,2,1,0:T(8,128)(2,1)}), bf16[8,2,16,512]{3,2,1,0:T(8,128)(2,1)S(1)}, u32[]{:S(2)}, u32[]{:S(2)}) %all-to-all-start) | async-done | bytes 262176 | tf_op jit(solution)/shard_map/all_to_all | solution.py:54
  45.2 1.8 %collective-permute-start.13 = (bf16[16,512]{1,0:T(8,128)(2,1)S(1)}, bf16[16,512]{1,0:T(8,128)(2,1)S(1)}, u32[]{:S(2)}, u32[]{:S(2)}) collective-permute-start(bf16[16,512]{1,0:T(8,128)(2,1)S(1)} %slice_reduce_fusion.a), channel_id=1, source_target_pairs={{0,64},{1,65},{2,66},{3,67},{4,68},{5,69},{6,70},{7,71},{8,72},{9,... | collective-permute-start | bytes 49160 | tf_op jit(solution)/shard_map/ppermute | solution.py:58
  47.0 1.3 %collective-permute-start.14 = (bf16[16,512]{1,0:T(8,128)(2,1)S(1)}, bf16[16,512]{1,0:T(8,128)(2,1)S(1)}, u32[]{:S(2)}, u32[]{:S(2)}) collective-permute-start(bf16[16,512]{1,0:T(8,128)(2,1)S(1)} %slice_reduce_fusion.a), channel_id=1, source_target_pairs={{0,192},{1,193},{2,194},{3,195},{4,196},{5,197},{6,198},{7,199},{8... | collective-permute-start | bytes 49160 | tf_op jit(solution)/shard_map/ppermute | solution.py:58
  48.3 1.1 %collective-permute-start.15 = (bf16[16,512]{1,0:T(8,128)(2,1)S(1)}, bf16[16,512]{1,0:T(8,128)(2,1)S(1)}, u32[]{:S(2)}, u32[]{:S(2)}) collective-permute-start(bf16[16,512]{1,0:T(8,128)(2,1)S(1)} %slice_reduce_fusion.a), channel_id=1, source_target_pairs={{0,128},{1,129},{2,130},{3,131},{4,132},{5,133},{6,134},{7,135},{8... | collective-permute-start | bytes 49160 | tf_op jit(solution)/shard_map/ppermute | solution.py:58
  49.4 3.9 %shard_map.108 = (bf16[1,1024,512]{2,1,0:T(8,128)(2,1)}, f32[1,16,512]{2,1,0:T(8,128)}) custom-call(bf16[16,2,16,512]{3,2,1,0:T(8,128)(2,1)S(1)} %bitcast.22, bf16[16,2,16,512]{3,2,1,0:T(8,128)(2,1)} %collective-permute-done.12.came_ref, bf16[8,2,16,512]{3,2,1,0:T(8,128)(2,1)S(1)} %all-to-all-done.pieces, bf16[1024,1024]{1,0:T(8,128)(2,1)S(1)} %shard_map.105.back), custom_call_target="tpu_custom_call" | custom-call | flops 1500000000 | bytes 1500000 | tf_op jit(solution)/shard_map/pallas_call | solution.py:85
  53.3 0.2 collective-permute-done.15.d
  53.5 0.8 %shard_map.109 = f32[16,512]{1,0:T(8,128)} custom-call(bf16[16,512]{1,0:T(8,128)(2,1)S(1)} %slice_reduce_fusion.a, bf16[16,512]{1,0:T(8,128)(2,1)S(1)} %collective-permute-done.13.b, bf16[16,512]{1,0:T(8,128)(2,1)S(1)} %collective-permute-done.14.c, bf16[16,512]{1,0:T(8,128)(2,1)S(1)} %collective-permute-done.15.d, bf16[512,512]{1,0:T(8,128)(2,1)S(1)} %get-tuple-element.64.factor), custom_call_target="tpu_custom_call" | custom-call | flops 30000000 | bytes 30000 | tf_op jit(solution)/shard_map/pallas_call | solution.py:85
  (18 shorter events, 0.2 us)
Async XLA Ops:
  1.5 12.3 %collective-permute-start = (bf16[64,512]{1,0:T(8,128)(2,1)S(1)}, bf16[64,512]{1,0:T(8,128)(2,1)S(1)}, u32[]{:S(2)}, u32[]{:S(2)}) collective-permute-start(bf16[64,512]{1,0:T(8,128)(2,1)S(1)} %get-tuple-element.37), channel_id=1, source_target_pairs={{0,56},{1,57},{2,58},{3,59},{4,60},{5,61},{6,62},{7,63},{8,48},{9,... | collective-permute-start | bytes 196616 | tf_op jit(solution)/shard_map/ppermute | solution.py:58
  7.5 6.3 %collective-permute-start.2 = (bf16[2,16,512]{2,1,0:T(8,128)(2,1)S(1)}, bf16[2,16,512]{2,1,0:T(8,128)(2,1)S(1)}, u32[]{:S(2)}, u32[]{:S(2)}) collective-permute-start(bf16[2,16,512]{2,1,0:T(8,128)(2,1)S(1)} %get-tuple-element.55), channel_id=1, source_target_pairs={{0,8},{1,9},{2,10},{3,11},{4,12},{5,13},{6,14},{7,15},{8,0},{9,1},... | collective-permute-start | bytes 98312 | tf_op jit(solution)/shard_map/ppermute | solution.py:58
  13.8 2.0 %collective-permute-start.3 = (bf16[4,2,4,16,512]{4,3,2,1,0:T(8,128)(2,1)S(1)}, bf16[4,2,4,16,512]{4,3,2,1,0:T(8,128)(2,1)S(1)}, u32[]{:S(2)}, u32[]{:S(2)}) collective-permute-start(bf16[4,2,4,16,512]{4,3,2,1,0:T(8,128)(2,1)S(1)} %get-tuple-element.44), channel_id=1, source_target_pairs={{0,1},{1,0},{2,3},{3,2},{4,5},{5,4},{6,7},{7,6},{8,9},{9,8},{10,11... | collective-permute-start | bytes 1572872 | tf_op jit(solution)/shard_map/ppermute | solution.py:58
  13.9 6.4 %collective-permute-start.9 = (bf16[2,2,16,512]{3,2,1,0:T(8,128)(2,1)S(1)}, bf16[2,2,16,512]{3,2,1,0:T(8,128)(2,1)S(1)}, u32[]{:S(2)}, u32[]{:S(2)}) collective-permute-start(bf16[2,2,16,512]{3,2,1,0:T(8,128)(2,1)S(1)} %pad_maximum_fusion.6), channel_id=1, source_target_pairs={{0,16},{1,17},{2,18},{3,19},{4,20},{5,21},{6,22},{7,23},{8,24},{9,... | collective-permute-start | bytes 196616 | tf_op jit(solution)/shard_map/ppermute | solution.py:58
  14.6 10.9 %collective-permute-start.1 = (bf16[2,64,512]{2,1,0:T(8,128)(2,1)S(1)}, bf16[2,64,512]{2,1,0:T(8,128)(2,1)S(1)}, u32[]{:S(2)}, u32[]{:S(2)}) collective-permute-start(bf16[2,64,512]{2,1,0:T(8,128)(2,1)S(1)} %pad_maximum_fusion.4), channel_id=1, source_target_pairs={{0,64},{1,65},{2,66},{3,67},{4,68},{5,69},{6,70},{7,71},{8,72},{9,... | collective-permute-start | bytes 393224 | tf_op jit(solution)/shard_map/ppermute | solution.py:58
  16.0 11.2 %collective-permute-start.5 = (bf16[2,4,16,512]{3,2,1,0:T(8,128)(2,1)S(1)}, bf16[2,4,16,512]{3,2,1,0:T(8,128)(2,1)S(1)}, u32[]{:S(2)}, u32[]{:S(2)}) collective-permute-start(bf16[2,4,16,512]{3,2,1,0:T(8,128)(2,1)S(1)} %get-tuple-element.49), channel_id=1, source_target_pairs={{0,4},{1,5},{2,6},{3,7},{4,0},{5,1},{6,2},{7,3},{8,12},{9,13},{10,... | collective-permute-start | bytes 393224 | tf_op jit(solution)/shard_map/ppermute | solution.py:58
  19.2 7.9 %collective-permute-start.6 = (bf16[2,4,16,512]{3,2,1,0:T(8,128)(2,1)S(1)}, bf16[2,4,16,512]{3,2,1,0:T(8,128)(2,1)S(1)}, u32[]{:S(2)}, u32[]{:S(2)}) collective-permute-start(bf16[2,4,16,512]{3,2,1,0:T(8,128)(2,1)S(1)} %get-tuple-element.50), channel_id=1, source_target_pairs={{0,2},{1,3},{2,0},{3,1},{4,6},{5,7},{6,4},{7,5},{8,10},{9,11},{10,... | collective-permute-start | bytes 393224 | tf_op jit(solution)/shard_map/ppermute | solution.py:58
  19.9 7.2 %collective-permute-start.7 = (bf16[2,4,16,512]{3,2,1,0:T(8,128)(2,1)S(1)}, bf16[2,4,16,512]{3,2,1,0:T(8,128)(2,1)S(1)}, u32[]{:S(2)}, u32[]{:S(2)}) collective-permute-start(bf16[2,4,16,512]{3,2,1,0:T(8,128)(2,1)S(1)} %get-tuple-element.51), channel_id=1, source_target_pairs={{0,6},{1,7},{2,4},{3,5},{4,2},{5,3},{6,0},{7,1},{8,14},{9,15},{10,... | collective-permute-start | bytes 393224 | tf_op jit(solution)/shard_map/ppermute | solution.py:58
  20.4 8.7 %collective-permute-start.10 = (bf16[2,2,2,16,512]{4,3,2,1,0:T(8,128)(2,1)S(1)}, bf16[2,2,2,16,512]{4,3,2,1,0:T(8,128)(2,1)S(1)}, u32[]{:S(2)}, u32[]{:S(2)}) collective-permute-start(bf16[2,2,2,16,512]{4,3,2,1,0:T(8,128)(2,1)S(1)} %pad_maximum_fusion.5), channel_id=1, source_target_pairs={{0,2},{1,3},{2,0},{3,1},{4,6},{5,7},{6,4},{7,5},{8,10},{9,11},{10,... | collective-permute-start | bytes 393224 | tf_op jit(solution)/shard_map/ppermute | solution.py:58
  25.5 8.9 %collective-permute-start.4 = (bf16[2,2,64,512]{3,2,1,0:T(8,128)(2,1)S(1)}, bf16[2,2,64,512]{3,2,1,0:T(8,128)(2,1)S(1)}, u32[]{:S(2)}, u32[]{:S(2)}) collective-permute-start(bf16[2,2,64,512]{3,2,1,0:T(8,128)(2,1)S(1)} %pad_maximum_fusion.2), channel_id=1, source_target_pairs={{0,192},{1,193},{2,194},{3,195},{4,196},{5,197},{6,198},{7,199},{8... | collective-permute-start | bytes 786440 | tf_op jit(solution)/shard_map/ppermute | solution.py:58
  29.1 8.9 %collective-permute-start.11 = (bf16[2,2,2,2,16,512]{5,4,3,2,1,0:T(8,128)(2,1)S(1)}, bf16[2,2,2,2,16,512]{5,4,3,2,1,0:T(8,128)(2,1)}, u32[]{:S(2)}, u32[]{:S(2)}) collective-permute-start(bf16[2,2,2,2,16,512]{5,4,3,2,1,0:T(8,128)(2,1)S(1)} %pad_maximum_fusion.3), channel_id=1, source_target_pairs={{0,6},{1,7},{2,4},{3,5},{4,2},{5,3},{6,0},{7,1},{8,14},{9,15},{10,... | collective-permute-start | bytes 786440 | tf_op jit(solution)/shard_map/ppermute | solution.py:58
  30.2 15.0 %all-to-all-start = ((bf16[8,2,16,512]{3,2,1,0:T(8,128)(2,1)}), bf16[8,2,16,512]{3,2,1,0:T(8,128)(2,1)S(1)}, u32[]{:S(2)}, u32[]{:S(2)}) async-start(bf16[8,2,16,512]{3,2,1,0:T(8,128)(2,1)} %shard_map.106), calls=%async_computation | async-start | bytes 524288 | tf_op jit(solution)/shard_map/all_to_all | solution.py:54
  34.5 4.8 %collective-permute-start.8 = (bf16[8,64,512]{2,1,0:T(8,128)(2,1)S(1)}, bf16[8,64,512]{2,1,0:T(8,128)(2,1)S(1)}, u32[]{:S(2)}, u32[]{:S(2)}) collective-permute-start(bf16[8,64,512]{2,1,0:T(8,128)(2,1)S(1)} %bitcast.19), channel_id=1, source_target_pairs={{0,1},{1,0},{2,3},{3,2},{4,5},{5,4},{6,7},{7,6},{8,9},{9,8},{10,11... | collective-permute-start | bytes 1572872 | tf_op jit(solution)/shard_map/ppermute | solution.py:58
  39.0 10.4 %collective-permute-start.12 = (bf16[16,2,16,512]{3,2,1,0:T(8,128)(2,1)S(1)}, bf16[16,2,16,512]{3,2,1,0:T(8,128)(2,1)}, u32[]{:S(2)}, u32[]{:S(2)}) collective-permute-start(bf16[16,2,16,512]{3,2,1,0:T(8,128)(2,1)S(1)} %bitcast.21), channel_id=1, source_target_pairs={{0,1},{1,0},{2,3},{3,2},{4,5},{5,4},{6,7},{7,6},{8,9},{9,8},{10,11... | collective-permute-start | bytes 1572872 | tf_op jit(solution)/shard_map/ppermute | solution.py:58
  45.2 8.1 %collective-permute-start.13 = (bf16[16,512]{1,0:T(8,128)(2,1)S(1)}, bf16[16,512]{1,0:T(8,128)(2,1)S(1)}, u32[]{:S(2)}, u32[]{:S(2)}) collective-permute-start(bf16[16,512]{1,0:T(8,128)(2,1)S(1)} %slice_reduce_fusion.a), channel_id=1, source_target_pairs={{0,64},{1,65},{2,66},{3,67},{4,68},{5,69},{6,70},{7,71},{8,72},{9,... | collective-permute-start | bytes 49160 | tf_op jit(solution)/shard_map/ppermute | solution.py:58
  47.0 6.3 %collective-permute-start.14 = (bf16[16,512]{1,0:T(8,128)(2,1)S(1)}, bf16[16,512]{1,0:T(8,128)(2,1)S(1)}, u32[]{:S(2)}, u32[]{:S(2)}) collective-permute-start(bf16[16,512]{1,0:T(8,128)(2,1)S(1)} %slice_reduce_fusion.a), channel_id=1, source_target_pairs={{0,192},{1,193},{2,194},{3,195},{4,196},{5,197},{6,198},{7,199},{8... | collective-permute-start | bytes 49160 | tf_op jit(solution)/shard_map/ppermute | solution.py:58
  48.3 5.2 %collective-permute-start.15 = (bf16[16,512]{1,0:T(8,128)(2,1)S(1)}, bf16[16,512]{1,0:T(8,128)(2,1)S(1)}, u32[]{:S(2)}, u32[]{:S(2)}) collective-permute-start(bf16[16,512]{1,0:T(8,128)(2,1)S(1)} %slice_reduce_fusion.a), channel_id=1, source_target_pairs={{0,128},{1,129},{2,130},{3,131},{4,132},{5,133},{6,134},{7,135},{8... | collective-permute-start | bytes 49160 | tf_op jit(solution)/shard_map/ppermute | solution.py:58
